TPU v7x, 32 devices: a whole 2x2x4 slice. The times are simulated.
32 devices in a mesh: dp: 16 (over z, y, x), tensor: 2 (over core).
Axes of the slice: x: 2, y: 2, z: 4, core: 2. Of those that a mesh axis runs over, the one named last changes fastest.
Arguments:
- tokens: bfloat16 [32, 1024, 768], P('dp'), may hold values from -6 to 6
- condition: bfloat16 [32, 128], P('dp'), may hold values from -6 to 6
- lengths: int32 [32], P('dp'), may hold values from 128 to 1024, as said below
- modulation_weight: bfloat16 [128, 4608], replicated, may hold values from -0.5 to 0.5
- modulation_bias: float32 [4608], replicated, may hold values from -3 to 3
- first_gain: float32 [768], replicated, may hold values from 0.5 to 1.5
- query_key_value_weight: bfloat16 [768, 3, 768], P(None, None, 'tensor'), may hold values from -0.21875 to 0.21875
- attention_out_weight: bfloat16 [768, 768], P('tensor'), may hold values from -1.25 to 1.25
- second_gain: float32 [768], replicated, may hold values from 0.5 to 1.5
- up_projection_weight: bfloat16 [768, 3072], P(None, 'tensor'), may hold values from -0.21875 to 0.21875
- upward_bias: float32 [3072], P('tensor'), may hold values from -2 to 2
- down_projection_weight: bfloat16 [3072, 768], P('tensor'), may hold values from -0.109375 to 0.109375
- downward_bias: float32 [768], replicated, may hold values from -2 to 2
- cotangent: bfloat16 [32, 1024, 768], P('dp', 'tensor'), may hold values from -6 to 6
Outputs:
- output: bfloat16 [32, 1024, 768], P('dp', 'tensor')
- grad_tokens: float32 [32, 1024, 768], P('dp', 'tensor')
- grad_condition: float32 [32, 128], P('dp')
- grad_modulation_weight: float32 [128, 4608], replicated
- grad_modulation_bias: float32 [4608], replicated
- grad_first_gain: float32 [768], replicated
- grad_input_weight: float32 [768, 3, 768], P(None, None, 'tensor')
- grad_output_weight: float32 [768, 768], P('tensor')
- grad_second_gain: float32 [768], replicated
- grad_upward_weight: float32 [768, 3072], P(None, 'tensor')
- grad_upward_bias: float32 [3072], P('tensor')
- grad_downward_weight: float32 [3072, 768], P('tensor')
- grad_downward_bias: float32 [768], replicated
Inputs may be any that keep to these rules, and one draw needn't show every extreme that they name: `lengths`: each sequence has 128, 512 or 1024 live slots, the first ones; every draw holds sequences of the shortest and of the full length.
All inputs are finite; a program needn't handle non-finite values.
Results may differ from a plain program's by a relative error of at most 0.012.
The roundings to bfloat16 on the way count: a program that leaves them out, or rounds other values in their place, can miss the bound.
Values may be sent and summed in bfloat16 or wider, within the bound.
No kernel may reach another device: no remote copies, remote signals or barrier semaphores. Data moves between devices by JAX's collectives and lax.ppermute only.
A program may use at most 192 MiB of HBM per device.

v0:
```python
from functools import partial

import jax
import jax.numpy as jnp
from jax import lax
from jax.sharding import PartitionSpec as P

HEAD = 64


def modulate(rows, gain, shift, scale):
    centre = jnp.mean(rows, axis=-1, keepdims=True)
    centred = rows - centre
    spread = jnp.mean(centred * centred, axis=-1, keepdims=True)
    normed = centred * lax.rsqrt(spread + 1e-05)
    return normed * gain * (1.0 + scale[:, None, :]) + shift[:, None, :]


def rotary_tables(full_span, head_size):
    half_size = head_size // 2
    frequency = 10000.0 ** (-(jnp.arange(half_size, dtype=jnp.float32) * 2.0 / head_size))
    angles = jnp.arange(full_span, dtype=jnp.float32)[:, None] * frequency[None, :]
    angles = jnp.concatenate([angles, angles], axis=1)
    return (jnp.cos(angles)[:, None, :], jnp.sin(angles)[:, None, :])


def rotate(values, cosine, sine):
    half_size = values.shape[-1] // 2
    turned = jnp.concatenate([-values[..., half_size:], values[..., :half_size]], axis=-1)
    return values * cosine + turned * sine


def masked_scores(queries, keys, length):
    scores = jnp.einsum("qhd,khd->hqk", queries, keys, preferred_element_type=jnp.float32)
    scores = scores * queries.shape[-1] ** (-0.5)
    live = jnp.arange(keys.shape[0]) < length
    return jnp.where(live[None, None, :], scores, -1e30)


def per_device(
    tokens,
    condition,
    lengths,
    modulation_weight,
    modulation_bias,
    first_gain,
    query_key_value_weight,
    attention_out_weight,
    second_gain,
    up_projection_weight,
    upward_bias,
    down_projection_weight,
    downward_bias,
    cotangent,
):
    sequences, full_span, features = tokens.shape
    local_width = query_key_value_weight.shape[2]
    head_count = local_width // HEAD
    half_rows = cotangent.shape[1]
    row_start = lax.axis_index("tensor") * half_rows
    block_rows = min(512, full_span)
    block_count = full_span // block_rows
    head_scale = HEAD ** (-0.5)
    cosine, sine = rotary_tables(full_span, HEAD)
    cond_float = condition.astype(jnp.float32)
    silu_values, silu_pull = jax.vjp(jax.nn.silu, cond_float)
    silu_cond = silu_values.astype(jnp.bfloat16)
    mods = (
        jnp.dot(silu_cond, modulation_weight, preferred_element_type=jnp.float32) + modulation_bias
    )
    mods = mods.reshape(sequences, 6, features)
    shift_one, scale_one, gate_one = (mods[:, 0], mods[:, 1], mods[:, 2])
    shift_two, scale_two, gate_two = (mods[:, 3], mods[:, 4], mods[:, 5])
    inputs = tokens.astype(jnp.float32)
    input_half = lax.dynamic_slice_in_dim(inputs, row_start, half_rows, 1)
    leading_rows = modulate(inputs, first_gain, shift_one, scale_one).astype(jnp.bfloat16)
    joined = jnp.einsum(
        "vpw,wux->vpux", leading_rows, query_key_value_weight, preferred_element_type=jnp.float32
    )

    def split_heads(values):
        return values.reshape(sequences, full_span, head_count, HEAD)

    def rotary(values):
        return rotate(values, cosine, sine)

    query_rot, query_pull = jax.vjp(rotary, split_heads(joined[:, :, 0]))
    key_rot, key_pull = jax.vjp(rotary, split_heads(joined[:, :, 1]))
    queries = query_rot.astype(jnp.bfloat16)
    keys = key_rot.astype(jnp.bfloat16)
    values = split_heads(joined[:, :, 2]).astype(jnp.bfloat16)

    def forward_sequence(element):
        query_seq, key_seq, value_seq, length = element

        def forward_one_block(query_block):
            scores = masked_scores(query_block, key_seq, length)
            highest = jnp.max(scores, axis=-1, keepdims=True)
            log_total = highest + jnp.log(
                jnp.sum(jnp.exp(scores - highest), axis=-1, keepdims=True)
            )
            probs_low = jnp.exp(scores - log_total).astype(jnp.bfloat16)
            result = jnp.einsum(
                "hqk,khd->qhd", probs_low, value_seq, preferred_element_type=jnp.float32
            )
            return (result, log_total)

        return lax.map(
            forward_one_block, query_seq.reshape(block_count, block_rows, head_count, HEAD)
        )

    attention_result, log_totals = lax.map(forward_sequence, (queries, keys, values, lengths))
    attention_result = attention_result.reshape(sequences, full_span, local_width).astype(
        jnp.bfloat16
    )
    branch_part = jnp.einsum(
        "gjo,oq->gjq", attention_result, attention_out_weight, preferred_element_type=jnp.float32
    )
    branch_one = lax.psum_scatter(branch_part, "tensor", scatter_dimension=1, tiled=True)
    middle = input_half + gate_one[:, None, :] * branch_one
    second_half, second_pull = jax.vjp(modulate, middle, second_gain, shift_two, scale_two)
    trailing_rows = lax.all_gather(second_half.astype(jnp.bfloat16), "tensor", axis=1, tiled=True)
    upper = jnp.einsum(
        "oui,ic->ouc", trailing_rows, up_projection_weight, preferred_element_type=jnp.float32
    )
    upper = upper + upward_bias
    activation_values, gelu_pull = jax.vjp(partial(jax.nn.gelu, approximate=True), upper)
    activation_values = activation_values.astype(jnp.bfloat16)
    mlp_part = jnp.einsum(
        "qgr,rx->qgx", activation_values, down_projection_weight, preferred_element_type=jnp.float32
    )
    branch_two = (
        lax.psum_scatter(
            mlp_part.astype(jnp.bfloat16), "tensor", scatter_dimension=1, tiled=True
        ).astype(jnp.float32)
        + downward_bias
    )
    output = (middle + gate_two[:, None, :] * branch_two).astype(jnp.bfloat16)
    upstream = cotangent.astype(jnp.float32)
    dgate_two = jnp.sum(upstream * branch_two, axis=1)
    grad_second_branch = (gate_two[:, None, :] * upstream).astype(jnp.bfloat16)
    grad_second_branch = lax.all_gather(grad_second_branch, "tensor", axis=1, tiled=True)
    grad_downward_bias = jnp.sum(grad_second_branch, axis=(0, 1), dtype=jnp.float32)
    grad_downward_weight = jnp.einsum(
        "eiu,eip->up", activation_values, grad_second_branch, preferred_element_type=jnp.float32
    )
    dactivated = jnp.einsum(
        "meu,tu->met",
        grad_second_branch,
        down_projection_weight,
        preferred_element_type=jnp.float32,
    )
    grad_upper_hidden = gelu_pull(dactivated)[0].astype(jnp.bfloat16)
    grad_upward_bias = jnp.sum(grad_upper_hidden, axis=(0, 1), dtype=jnp.float32)
    grad_upward_weight = jnp.einsum(
        "tyv,tye->ve", trailing_rows, grad_upper_hidden, preferred_element_type=jnp.float32
    )
    dsecond_part = jnp.einsum(
        "ipy,zy->ipz", grad_upper_hidden, up_projection_weight, preferred_element_type=jnp.float32
    )
    dsecond = lax.psum_scatter(dsecond_part, "tensor", scatter_dimension=1, tiled=True)
    dmiddle_norm, grad_second_gain, dshift_two, dscale_two = second_pull(dsecond)
    dmiddle = upstream + dmiddle_norm
    dgate_one = jnp.sum(dmiddle * branch_one, axis=1)
    grad_first_branch = (gate_one[:, None, :] * dmiddle).astype(jnp.bfloat16)
    grad_first_branch = lax.all_gather(grad_first_branch, "tensor", axis=1, tiled=True)
    grad_output_weight = jnp.einsum(
        "vmo,vmt->ot", attention_result, grad_first_branch, preferred_element_type=jnp.float32
    )
    dattended = jnp.einsum(
        "bpf,jf->bpj", grad_first_branch, attention_out_weight, preferred_element_type=jnp.float32
    )
    dattended = split_heads(dattended.astype(jnp.bfloat16))

    def backward_sequence(element):
        query_seq, key_seq, value_seq, grad_seq, total_seq, length = element

        def backward_one_block(carry, pieces):
            query_block, grad_block, total_block = pieces
            scores = masked_scores(query_block, key_seq, length)
            probs = jnp.exp(scores - total_block)
            dvalue = jnp.einsum(
                "hqk,qhd->khd",
                probs.astype(jnp.bfloat16),
                grad_block,
                preferred_element_type=jnp.float32,
            )
            dprobs = jnp.einsum(
                "qhd,khd->hqk", grad_block, value_seq, preferred_element_type=jnp.float32
            )
            weighted = jnp.sum(probs * dprobs, axis=-1, keepdims=True)
            dscores = (probs * (dprobs - weighted)).astype(jnp.bfloat16)
            dquery = (
                jnp.einsum("hqk,khd->qhd", dscores, key_seq, preferred_element_type=jnp.float32)
                * head_scale
            )
            dkey = (
                jnp.einsum("hqk,qhd->khd", dscores, query_block, preferred_element_type=jnp.float32)
                * head_scale
            )
            dquery, dkey, dvalue = (dquery, dkey, dvalue)
            return ((carry[0] + dkey, carry[1] + dvalue), dquery)

        empty = jnp.zeros((full_span, head_count, HEAD), jnp.float32)
        pieces = (
            query_seq.reshape(block_count, block_rows, head_count, HEAD),
            grad_seq.reshape(block_count, block_rows, head_count, HEAD),
            total_seq,
        )
        (dkey, dvalue), dquery = lax.scan(backward_one_block, (empty, empty), pieces)
        return (dquery.reshape(full_span, head_count, HEAD), dkey, dvalue)

    dqueries, dkeys, dvalues = lax.map(
        backward_sequence, (queries, keys, values, dattended, log_totals, lengths)
    )
    grad_joined_heads = jnp.stack(
        [
            query_pull(dqueries)[0].reshape(sequences, full_span, local_width),
            key_pull(dkeys)[0].reshape(sequences, full_span, local_width),
            dvalues.reshape(sequences, full_span, local_width),
        ],
        axis=2,
    ).astype(jnp.bfloat16)
    grad_input_weight = jnp.einsum(
        "uvt,uvwb->twb", leading_rows, grad_joined_heads, preferred_element_type=jnp.float32
    )
    dfirst_part = jnp.einsum(
        "iwnb,mnb->iwm",
        grad_joined_heads,
        query_key_value_weight,
        preferred_element_type=jnp.float32,
    )
    dfirst = lax.psum_scatter(dfirst_part, "tensor", scatter_dimension=1, tiled=True)
    first_half, first_pull = jax.vjp(modulate, input_half, first_gain, shift_one, scale_one)
    dinput_norm, grad_first_gain, dshift_one, dscale_one = first_pull(dfirst)
    grad_tokens = dmiddle + dinput_norm
    dmods = jnp.stack(
        [dshift_one, dscale_one, dgate_one, dshift_two, dscale_two, dgate_two], axis=1
    )
    dmods, grad_first_gain, grad_second_gain = lax.psum(
        (dmods, grad_first_gain, grad_second_gain), "tensor"
    )
    dmods_low = dmods.reshape(sequences, 6 * features).astype(jnp.bfloat16)
    grad_modulation_bias = jnp.sum(dmods_low, axis=0, dtype=jnp.float32)
    grad_modulation_weight = jnp.dot(silu_cond.T, dmods_low, preferred_element_type=jnp.float32)
    dsilu = jnp.dot(dmods_low, modulation_weight.T, preferred_element_type=jnp.float32)
    grad_condition = silu_pull(dsilu)[0]
    (
        grad_modulation_weight,
        grad_modulation_bias,
        grad_first_gain,
        grad_input_weight,
        grad_output_weight,
        grad_second_gain,
        grad_upward_weight,
        grad_upward_bias,
        grad_downward_weight,
        grad_downward_bias,
    ) = lax.psum(
        (
            grad_modulation_weight,
            grad_modulation_bias,
            grad_first_gain,
            grad_input_weight,
            grad_output_weight,
            grad_second_gain,
            grad_upward_weight,
            grad_upward_bias,
            grad_downward_weight,
            grad_downward_bias,
        ),
        "dp",
    )
    return (
        output,
        grad_tokens,
        grad_condition,
        grad_modulation_weight,
        grad_modulation_bias,
        grad_first_gain,
        grad_input_weight,
        grad_output_weight,
        grad_second_gain,
        grad_upward_weight,
        grad_upward_bias,
        grad_downward_weight,
        grad_downward_bias,
    )


def solution(mesh):
    placed = (
        P("dp", None, None),
        P("dp", None),
        P("dp"),
        P(),
        P(),
        P(),
        P(None, None, "tensor"),
        P("tensor", None),
        P(),
        P(None, "tensor"),
        P("tensor"),
        P("tensor", None),
        P(),
        P("dp", "tensor", None),
    )
    return jax.shard_map(
        per_device,
        mesh=mesh,
        in_specs=placed,
        out_specs=(
            P("dp", "tensor", None),
            P("dp", "tensor", None),
            P("dp", None),
            P(),
            P(),
            P(),
            P(None, None, "tensor"),
            P("tensor", None),
            P(),
            P(None, "tensor"),
            P("tensor"),
            P("tensor", None),
            P(),
        ),
        check_vma=False,
    )
```

profile of v0, /device:TPU:0, one launch (start us, length us, event | category | flops | bytes accessed | tf_op | source)
XLA Modules:
  0.0 963.9 jit_solution(3136590563258978081)
XLA Ops:
  12.4 7.5 fusion.60
  33.8 87.5 %while.54 = (s32[]{:T(128)}, bf16[2,2,512,6,64]{2,4,3,1,0:T(8,128)(2,1)}, f32[2,2,6,512,1]{3,2,1,4,0:T(8,128)S(1)}, bf16[2,1024,6,64]{1,3,2,0:T(8,128)(2,1)}, bf...) while((s32[]{:T(128)}, ...), condition=%wide.region_7.8_spmd, body=%wide.region_2.7_spmd.sunk | while | flops 839907328 | bytes 109896088 | solution.py:112
  42.7 32.9 %while.57 = (s32[]{:T(128)}, bf16[2,512,6,64]{1,3,2,0:T(8,128)(2,1)}, f32[2,6,512,1]{2,1,3,0:T(8,128)S(1)}, s32[]{:T(128)}, bf16[2,512,6,64]{1,3,2,0:T(8,128)(2,...) while((s32[]{:T(128)}, bf16[2,512,6,64]{1,3,2,0:T(8,128)(2,1)}, ...), condition=%wide.region_6.6_spmd, body=%wide.region_3.5_spmd.sunk | while | flops 839907328 | bytes 100393168 | solution.py:108
  51.0 7.2 fusion.143
  67.5 7.2 fusion.143
  86.3 32.9 %while.57 = (s32[]{:T(128)}, bf16[2,512,6,64]{1,3,2,0:T(8,128)(2,1)}, f32[2,6,512,1]{2,1,3,0:T(8,128)S(1)}, s32[]{:T(128)}, bf16[2,512,6,64]{1,3,2,0:T(8,128)(2,...) while((s32[]{:T(128)}, bf16[2,512,6,64]{1,3,2,0:T(8,128)(2,1)}, ...), condition=%wide.region_6.6_spmd, body=%wide.region_3.5_spmd.sunk | while | flops 839907328 | bytes 100393168 | solution.py:108
  94.7 7.2 fusion.143
  111.1 7.2 fusion.143
  140.9 11.8 %reduce-scatter.5.cloned.1.call-done = f32[2,512,768]{2,1,0:T(8,128)} async-done(((f32[2,1024,768]{2,1,0:T(8,128)}), f32[2,512,768]{2,1,0:T(8,128)}) %reduce-scatter.5.cloned.1.call-update) | async-done | bytes 3145744 | tf_op jit(solution)/shard_map/reduce_scatter | solution.py:119
  163.2 10.5 %all-gather.4.cloned.1.call-done = bf16[2,1024,768]{2,1,0:T(8,128)(2,1)} async-done(((bf16[2,512,768]{2,1,0:T(8,128)(2,1)}), bf16[2,1024,768]{2,1,0:T(8,128)(2,1)}) %all-gather.4.cloned.1.call-update) | async-done | bytes 3145744 | tf_op jit(solution)/shard_map/all_gather | solution.py:122
  173.7 13.8 %multiply_convert_fusion.1 = (bf16[2,1024,1536]{2,1,0:T(8,128)(2,1)}, f32[2,1024,1536]{2,1,0:T(8,128)}) fusion(f32[1536]{0:T(1024)S(1)} %copy-done.75, bf16[2,1024,768]{2,1,0:T(8,128)(2,1)} %all-gather.4.cloned.1.call-done, bf16[768,1536]{1,0:T(8,128)(2,1)S(1)} %copy-done), kind=kOutput, calls=%fused_computation.69 | convolution fusion | flops 4863295488 | bytes 24385536 | tf_op jit(solution)/shard_map/oui,ic->ouc/dot_general | solution.py:123
  189.2 17.3 %convert_reduce_fusion = (f32[1536]{0:T(1024)}, bf16[2,1024,1536]{2,1,0:T(8,128)(2,1)S(1)}) fusion(f32[2,1024,1536]{2,1,0:T(8,128)} %get-tuple-element.443, f32[1536]{0:T(1024)S(1)} %copy-done.75, bf16[2,1024,768]{2,1,0:T(8,128)(2,1)} %all-gather.6.cloned.1.call-done, bf16[1536,768]{1,0:T(8,128)(2,1)} %param.33), kind=kOutput, calls=%fused_computation.68 | convolution fusion | flops 4904188416 | bytes 24391680 | tf_op jit(solution)/shard_map/meu,tu->met/dot_general | solution.py:147
  209.2 7.0 fusion.52
  217.8 9.2 fusion.56
  236.3 10.4 %reduce-scatter.7.cloned.1.call-done = bf16[2,512,768]{2,1,0:T(8,128)(2,1)} async-done(((bf16[2,1024,768]{2,1,0:T(8,128)(2,1)}), bf16[2,512,768]{2,1,0:T(8,128)(2,1)}) %reduce-scatter.7.cloned.1.call-update) | async-done | bytes 1572880 | tf_op jit(solution)/shard_map/reduce_scatter | solution.py:133
  255.1 13.4 %all-gather.8.cloned.1.call-done = bf16[2,1024,768]{2,1,0:T(8,128)(2,1)} async-done(((bf16[2,512,768]{2,1,0:T(8,128)(2,1)}), bf16[2,1024,768]{2,1,0:T(8,128)(2,1)}) %all-gather.8.cloned.1.call-update) | async-done | bytes 3145744 | tf_op jit(solution)/shard_map/all_gather | solution.py:166
  272.9 134.4 %while.56 = (s32[]{:T(128)}, f32[2,1024,6,64]{1,3,2,0:T(8,128)}, f32[2,1024,6,64]{1,3,2,0:T(8,128)}, bf16[2,1024,6,64]{1,3,2,0:T(8,128)(2,1)}, bf16[2,1024,6,64]...) while((s32[]{:T(128)}, f32[2,1024,6,64]{1,3,2,0:T(8,128)}, ...), condition=%wide.region_19.20_spmd, body=%wide.region_15.19_spmd.sunk | while | flops 2062612480 | bytes 190858144 | solution.py:213
  280.5 46.5 %while.58 = (s32[]{:T(128)}, f32[1024,6,64]{0,2,1:T(8,128)S(1)}, f32[1024,6,64]{0,2,1:T(8,128)}, f32[2,512,6,64]{1,3,2,0:T(8,128)}, bf16[2,512,6,64]{1,3,2,0:T(8...) while((s32[]{:T(128)}, f32[1024,6,64]{0,2,1:T(8,128)S(1)}, ...), condition=%wide.region_18.18_spmd.clone, body=%wide.region_16.17_spmd.clone.sunk | while | flops 2062612480 | bytes 136937808 | solution.py:210
  286.1 6.5 multiply_reduce_fusion.12
  292.6 6.6 multiply_convert_fusion.4
  309.4 6.5 multiply_reduce_fusion.12
  315.9 6.6 multiply_convert_fusion.4
  347.5 46.6 %while.58 = (s32[]{:T(128)}, f32[1024,6,64]{0,2,1:T(8,128)S(1)}, f32[1024,6,64]{0,2,1:T(8,128)}, f32[2,512,6,64]{1,3,2,0:T(8,128)}, bf16[2,512,6,64]{1,3,2,0:T(8...) while((s32[]{:T(128)}, f32[1024,6,64]{0,2,1:T(8,128)S(1)}, ...), condition=%wide.region_18.18_spmd.clone, body=%wide.region_16.17_spmd.clone.sunk | while | flops 2062612480 | bytes 136937808 | solution.py:210
  353.1 6.5 multiply_reduce_fusion.12
  359.6 6.6 multiply_convert_fusion.4
  382.9 6.6 multiply_convert_fusion.4
  425.8 9.9 %convolution_bitcast_fusion.2 = f32[2,1024,768]{2,1,0:T(8,128)} fusion(bf16[2,1024,1,384]{3,1,2,0:T(8,128)(2,1)} %copy.75, bf16[2,1024,1,384]{3,1,2,0:T(8,128)(2,1)} %copy.74, bf16[2,1024,1,384]{3,1,2,0:T(8,128)(2,1)} %copy.73, bf16[768,3,384]{2,0,1:T(8,128)(2,1)} %param.28), kind=kOutput, calls=%fused_computation.112 | convolution fusion | flops 3628597248 | bytes 12779520 | tf_op jit(solution)/shard_map/iwnb,mnb->iwm/dot_general | solution.py:227
  436.4 9.8 %convolution_bitcast_fusion.1 = f32[768,1536]{1,0:T(8,128)} fusion(bf16[2,1024,768]{2,1,0:T(8,128)(2,1)} %all-gather.4.cloned.1.call-done, bf16[2,1024,1536]{2,1,0:T(8,128)(2,1)} %copy-done.79), kind=kOutput, calls=%fused_computation.82 | convolution fusion | flops 4831838208 | bytes 14155776 | tf_op jit(solution)/shard_map/tyv,tye->ve/dot_general | solution.py:155
  446.2 9.8 %convolution_bitcast_fusion = f32[1536,768]{1,0:T(8,128)} fusion(bf16[2,1024,1536]{2,1,0:T(8,128)(2,1)} %get-tuple-element.442, bf16[2,1024,768]{2,1,0:T(8,128)(2,1)S(1)} %copy-done.32), kind=kOutput, calls=%fused_computation.81 | convolution fusion | flops 4831838208 | bytes 14155776 | tf_op jit(solution)/shard_map/eiu,eip->up/dot_general | solution.py:144
  459.4 6.6 convolution_bitcast_fusion.3
  487.0 82.0 %all-reduce.4 = (f32[4608]{0:T(1024)}, f32[768]{0:T(1024)}, f32[768]{0:T(1024)}, f32[1536]{0:T(1024)}, f32[768]{0:T(1024)}) all-reduce(f32[4608]{0:T(1024)S(1)} %reduce_sum.266, f32[768]{0:T(1024)S(1)} %get-tuple-element.397, f32[768]{0:T(1024)S(1)} %get-tuple-element.398, ...), channel_id=1, replica_groups=mesh['dp'=16,'tensor'=2] {'dp'}, use_global_device_ids=true, to_apply=%region_34.35 | all-reduce | flops 8448 | bytes 67584 | tf_op jit(solution)/shard_map/psum | solution.py:259
  570.0 373.7 %all-reduce.9.cloned.1.call-done = (f32[128,4608]{1,0:T(8,128)}, f32[768,3,384]{2,0,1:T(8,128)}, f32[384,768]{1,0:T(8,128)}, f32[768,1536]{1,0:T(8,128)}, f32[1536,768]{1,0:T(8,128)}) async-done(((f32[128,4608]{1,0:T(8,128)}, f32[768,3,384]{2,0,1:T(8,128)}, f32[384,768]{1,0:T(8,128)}, f32[768,1536]{1,0:T(8,128)}, f32[1536,768]{1,0:T(8,128)}), (f32[128,4608]{1,0:T(8,128)}, f32[768,3,384]{2,0,1:T(8,128)}, ...) | async-done | bytes 16515088 | tf_op jit(solution)/shard_map/psum | solution.py:259
  (429 shorter events, 279.8 us)
Async XLA Ops:
  7.2 166.5 %copy-start = (bf16[768,1536]{1,0:T(8,128)(2,1)S(1)}, bf16[768,1536]{1,0:T(8,128)(2,1)}, u32[]{:S(2)}) copy-start(bf16[768,1536]{1,0:T(8,128)(2,1)} %param.31) | copy-start | bytes 7077892
  7.2 145.5 %reduce-scatter.5.cloned.1.call-start = ((), (), s32[]{:S(2)}) async-start(), calls=%async_computation.4 | async-start | bytes 9437184 | tf_op jit(solution)/shard_map/reduce_scatter | solution.py:119
  7.3 5.1 copy-start.51
  10.3 9.6 copy-start.53
  11.4 8.5 copy-start.67
  12.4 7.6 copy-start.46
  12.4 7.6 copy-start.69
  121.3 8.0 copy-start.43
  135.3 38.3 %all-gather.4.cloned.1.call-start = ((), (), s32[]{:S(2)}) async-start(), calls=%async_computation.5 | async-start | bytes 4718592 | tf_op jit(solution)/shard_map/all_gather | solution.py:122
  135.8 5.0 copy-start.60
  160.2 13.5 %copy-start.75 = (f32[1536]{0:T(1024)S(1)}, f32[1536]{0:T(1024)}, u32[]{:S(2)}) copy-start(f32[1536]{0:T(1024)} %param.32) | copy-start | bytes 18436
  160.2 29.0 %all-gather.6.cloned.1.call-start = ((), (), s32[]{:S(2)}) async-start(), calls=%async_computation.7 | async-start | bytes 4718592 | tf_op jit(solution)/shard_map/all_gather | solution.py:142
  163.1 68.8 %reduce-scatter.9.cloned.1.call-start = ((), (), s32[]{:S(2)}) async-start(), calls=%async_computation.8 | async-start | bytes 9437184 | tf_op jit(solution)/shard_map/reduce_scatter | solution.py:161
  216.1 30.6 %reduce-scatter.7.cloned.1.call-start = ((), (), s32[]{:S(2)}) async-start(), calls=%async_computation.6 | async-start | bytes 4718592 | tf_op jit(solution)/shard_map/reduce_scatter | solution.py:133
  227.0 19.7 %copy-start.62 = (f32[768]{0:T(1024)S(1)}, f32[768]{0:T(1024)}, u32[]{:S(2)}) copy-start(f32[768]{0:T(1024)} %param.34) | copy-start | bytes 9220
  227.0 41.5 %all-gather.8.cloned.1.call-start = ((), (), s32[]{:S(2)}) async-start(), calls=%async_computation.9 | async-start | bytes 4718592 | tf_op jit(solution)/shard_map/all_gather | solution.py:166
  236.3 17.0 %copy-start.21 = (bf16[2,512,768]{2,1,0:T(8,128)(2,1)S(1)}, bf16[2,512,768]{2,1,0:T(8,128)(2,1)}, u32[]{:S(2)}) copy-start(bf16[2,512,768]{2,1,0:T(8,128)(2,1)} %param.35) | copy-start | bytes 4718596
  255.0 211.0 %reduce-scatter.11.cloned.1.call-start = ((), (), s32[]{:S(2)}) async-start(), calls=%async_computation.10 | async-start | bytes 9437184 | tf_op jit(solution)/shard_map/reduce_scatter | solution.py:233
  286.1 6.5 copy-start.9
  309.4 6.5 copy-start.9
  353.1 6.5 copy-start.9
  376.4 6.5 copy-start.9
  435.8 508.0 %all-reduce.9.cloned.1.call-start = ((), (), s32[]{:S(2)}) async-start(), calls=%async_computation.11 | async-start | bytes 33030144 | tf_op jit(solution)/shard_map/psum | solution.py:259
  436.4 9.8 %copy-start.32 = (bf16[2,1024,768]{2,1,0:T(8,128)(2,1)S(1)}, bf16[2,1024,768]{2,1,0:T(8,128)(2,1)}, u32[]{:S(2)}) copy-start(bf16[2,1024,768]{2,1,0:T(8,128)(2,1)} %all-gather.6.cloned.1.call-done) | copy-start | bytes 9437188
  446.2 9.9 %copy-start.27 = (bf16[2,1024,384]{1,2,0:T(8,128)(2,1)S(1)}, bf16[2,1024,384]{1,2,0:T(8,128)(2,1)}, u32[]{:S(2)}) copy-start(bf16[2,1024,384]{1,2,0:T(8,128)(2,1)} %convert_element_type.93) | copy-start | bytes 4718596
  446.2 9.9 %copy-start.73 = (bf16[2,1024,768]{2,1,0:T(8,128)(2,1)S(1)}, bf16[2,1024,768]{2,1,0:T(8,128)(2,1)}, u32[]{:S(2)}) copy-start(bf16[2,1024,768]{2,1,0:T(8,128)(2,1)} %all-gather.8.cloned.1.call-done) | copy-start | bytes 9437188
  446.2 12.4 %copy-start.39 = (bf16[2,1024,1,384]{3,1,2,0:T(8,128)(2,1)S(1)}, bf16[2,1024,1,384]{3,1,2,0:T(8,128)(2,1)}, u32[]{:S(2)}) copy-start(bf16[2,1024,1,384]{3,1,2,0:T(8,128)(2,1)} %copy.74) | copy-start | bytes 4718596
  466.0 7.8 copy-start.23
  474.0 8.4 copy-start.72
  484.4 84.6 %copy-start.30 = (bf16[128,4608]{1,0:T(8,128)(2,1)S(1)}, bf16[128,4608]{1,0:T(8,128)(2,1)}, u32[]{:S(2)}) copy-start(bf16[128,4608]{1,0:T(8,128)(2,1)} %param.25) | copy-start | bytes 3538948
  943.8 7.4 slice-start.2
  951.2 5.7 copy-start.1
  (98 other events, 297.0 us)
Sparse Core Ops, SparseCore 0:
  135.4 17.1 reduce-scatter.4
  160.3 13.2 all-gather.3
  175.8 13.2 all-gather.5
  216.3 15.6 reduce-scatter.8
  234.6 12.0 reduce-scatter.6
  255.1 13.2 all-gather.7
  435.9 15.6 reduce-scatter.10
  484.5 459.1 all-reduce.8
where the time goes:
time: 971 us; the launch traced here: 964 us
  waiting for transfers between devices  427 us (44%)
  matrix products  206 us (21%)
  local copies, waits for them, and re-layouts  123 us (13%)
  other arithmetic  104 us (11%)
  blocking collectives  85.6 us (9%)
  between operations  15.1 us (2%)
    psum x1, waiting for transfers between devices, per_device(): lax.psum((grad_modulation_weight, grad_modulation_bias, grad_first_gain,...  374 us
    psum x1, blocking collectives, per_device(): lax.psum((grad_modulation_weight, grad_modulation_bias, grad_first_gain,...  82 us
    dot_general x4, matrix products, forward_one_block(): jnp.einsum('hqk,khd->qhd', probs_low, value_seq, preferred_element_type=j...  28.9 us
    convert_element_type x4, other arithmetic, backward_one_block(): dscores = (probs * (dprobs - weighted)).astype(jnp.bfloat16)  26.3 us
    unnamed x146, local copies, waits for them, and re-layouts  26.1 us
    dot_general x4, matrix products, backward_one_block(): jnp.einsum('qhd,khd->hqk', grad_block, value_seq, preferred_element_type=...  25.9 us
    while x116, local copies, waits for them, and re-layouts  20 us
  transfers between devices with their start and end apart: 8, of which 7 were waited for; matrix products, arithmetic and copies ran while one was open for 7% of the time, Pallas kernels for 0%

commit v1 on v0

v1 whole, which is shorter than its diff:
```python
import math
from functools import partial

import jax
import jax.numpy as jnp
import numpy as np
from jax import lax
from jax.experimental import pallas as pl
from jax.experimental.pallas import tpu as pltpu
from jax.sharding import PartitionSpec as P

HEAD = 64
HALF = HEAD // 2
EPS = 1e-05
LOG2_SCALE = math.log2(math.e) * HEAD ** (-0.5)
SAFE_BOUND = 70.0
GELU_A = math.sqrt(2.0 / math.pi)
GELU_B = 0.044715
BF = jnp.bfloat16
F32 = jnp.float32

NN = (((1,), (0,)), ((), ()))
NT = (((1,), (1,)), ((), ()))
TN = (((0,), (0,)), ((), ()))
TT = (((0,), (1,)), ((), ()))
dot = partial(lax.dot_general, preferred_element_type=F32)


def call(body, grid, in_specs, out_specs, out_shape, flops, scratch=(), prefetch=0, vmem=56):
    moved = sum(math.prod(s.shape) * s.dtype.itemsize for s in out_shape)
    return pl.pallas_call(
        body,
        grid_spec=pltpu.PrefetchScalarGridSpec(
            num_scalar_prefetch=prefetch,
            grid=grid,
            in_specs=in_specs,
            out_specs=out_specs,
            scratch_shapes=list(scratch),
        ),
        out_shape=out_shape,
        compiler_params=pltpu.CompilerParams(vmem_limit_bytes=vmem * 2**20),
        cost_estimate=pl.CostEstimate(
            flops=int(flops), bytes_accessed=int(2 * moved), transcendentals=0
        ),
    )


def shaped(shape, dtype):
    return jax.ShapeDtypeStruct(shape, dtype)


def rotary_tables(span):
    frequency = (
        np.float32(10000.0) ** (-(np.arange(HALF, dtype=np.float32) * np.float32(2.0 / HEAD)))
    ).astype(np.float32)
    angles = (np.arange(span, dtype=np.float32)[None, :] * frequency[:, None]).astype(np.float32)
    angles = angles.astype(np.float64)
    return np.cos(angles).astype(np.float32), np.sin(angles).astype(np.float32)


def normed_rows(rows):
    centre = jnp.mean(rows, axis=-1, keepdims=True)
    centred = rows - centre
    spread = jnp.mean(centred * centred, axis=-1, keepdims=True)
    inverse = lax.rsqrt(spread + EPS)
    return centred * inverse, inverse


def project(source, weight, vectors, cosine, sine, first):
    span, features = source.shape
    _, _, width = weight.shape

    def body(source_ref, weight_ref, vector_ref, cos_ref, sin_ref, *rest):
        if first:
            rows_ref, out_ref = rest

            @pl.when(pl.program_id(0) == 0)
            def _():
                for start in range(0, span, 128):
                    hat, _ = normed_rows(source_ref[start : start + 128, :].astype(F32))
                    rows_ref[start : start + 128, :] = (
                        hat * vector_ref[0:1, :] + vector_ref[1:2, :]
                    ).astype(BF)
        else:
            (out_ref,) = rest
            rows_ref = source_ref
        joined = dot(weight_ref[0], rows_ref[...], TT)

        @pl.when(pl.program_id(0) < 2)
        def _():
            cos, sin = cos_ref[...], sin_ref[...]
            for at in range(0, width, HEAD):
                low, high = joined[at : at + HALF], joined[at + HALF : at + HEAD]
                out_ref[0, at : at + HALF, :] = (low * cos - high * sin).astype(BF)
                out_ref[0, at + HALF : at + HEAD, :] = (high * cos + low * sin).astype(BF)

        @pl.when(pl.program_id(0) == 2)
        def _():
            out_ref[0] = joined.astype(BF)

    whole = lambda c: (0, 0)
    out_specs = [pl.BlockSpec((1, width, span), lambda c: (c, 0, 0))]
    out_shape = [shaped((3, width, span), BF)]
    if first:
        out_specs = [pl.BlockSpec((span, features), whole)] + out_specs
        out_shape = [shaped((span, features), BF)] + out_shape
    return call(
        body,
        (3,),
        [
            pl.BlockSpec((span, features), whole),
            pl.BlockSpec((1, features, width), lambda c: (c, 0, 0)),
            pl.BlockSpec(vectors.shape, whole),
            pl.BlockSpec(cosine.shape, whole),
            pl.BlockSpec(sine.shape, whole),
        ],
        out_specs,
        out_shape,
        6 * span * features * width,
    )(source, weight, vectors, cosine, sine)


def live_lengths(span):
    return (span, span // 2, span // 8)


def attend(length, joined):
    _, width, span = joined.shape
    per_step = 2
    query_block = min(512, span)

    def one_length(live, query_ref, key_ref, value_ref, out_ref, total_ref):
        key_block = min(512, live)
        for head in range(per_step):
            at = slice(head * HEAD, (head + 1) * HEAD)
            keys = key_ref[0, at, :live].T
            query_size = jnp.sum(jnp.square(query_ref[0, at, :].astype(F32)), axis=0)
            key_size = jnp.sum(jnp.square(key_ref[0, at, :live].astype(F32)), axis=0)
            largest = jnp.max(query_size) * jnp.max(key_size)
            safe = largest < (SAFE_BOUND / HEAD ** (-0.5)) ** 2

            @pl.when(safe)
            def _():
                for first in range(0, span, query_block):
                    columns = slice(first, first + query_block)
                    queries = query_ref[0, at, columns]
                    result = jnp.zeros((HEAD, query_block), F32)
                    total = jnp.zeros((1, query_block), F32)
                    for start in range(0, live, key_block):
                        rows = slice(start, start + key_block)
                        probs = jnp.exp2(dot(keys[rows], queries, NN) * LOG2_SCALE)
                        total = total + jnp.sum(probs, axis=0, keepdims=True)
                        result = result + dot(value_ref[0, at, rows], probs.astype(BF), NN)
                    out_ref[at, columns] = (result * (1.0 / total)).astype(BF)
                    total_ref[0, head : head + 1, columns] = jnp.log2(total)

            @pl.when(jnp.logical_not(safe))
            def _():
                for first in range(0, span, query_block):
                    columns = slice(first, first + query_block)
                    scores = dot(keys, query_ref[0, at, columns], NN) * LOG2_SCALE
                    highest = jnp.max(scores, axis=0, keepdims=True)
                    probs = jnp.exp2(scores - highest)
                    total = jnp.sum(probs, axis=0, keepdims=True)
                    result = dot(value_ref[0, at, :live], probs.astype(BF), NN)
                    out_ref[at, columns] = (result * (1.0 / total)).astype(BF)
                    total_ref[0, head : head + 1, columns] = highest + jnp.log2(total)

    def body(length_ref, query_ref, key_ref, value_ref, out_ref, total_ref):
        for live in live_lengths(span):

            @pl.when(length_ref[0] == live)
            def _():
                one_length(live, query_ref, key_ref, value_ref, out_ref, total_ref)

    rows = per_step * HEAD

    def part(c):
        return pl.BlockSpec((1, rows, span), lambda i, n: (c, i, 0))

    return call(
        body,
        (width // rows,),
        [part(0), part(1), part(2)],
        [
            pl.BlockSpec((rows, span), lambda i, n: (i, 0)),
            pl.BlockSpec((1, per_step, span), lambda i, n: (i, 0, 0)),
        ],
        [shaped((width, span), BF), shaped((width // rows, per_step, span), F32)],
        16 * span * span * width,
        prefetch=1,
    )(length, joined, joined, joined)


def attend_back(length, joined, attended, dattended, totals, cosine, sine):
    _, width, span = joined.shape
    per_step = 2
    key_block_most = 256

    def turned(grads, cos, sin, out_ref, part, head, columns):
        low, high = grads[:HALF], grads[HALF:]
        top = head * HEAD
        out_ref[part, top : top + HALF, columns] = (low * cos + high * sin).astype(BF)
        out_ref[part, top + HALF : top + HEAD, columns] = (high * cos - low * sin).astype(BF)

    def one_length(live, query_ref, key_ref, value_ref, out_ref, dout_ref, total_ref, cos_ref, sin_ref, grad_ref):
        key_block = min(key_block_most, live)
        for head in range(per_step):
            at = slice(head * HEAD, (head + 1) * HEAD)
            keys = key_ref[0, at, :live].T
            values = value_ref[0, at, :live].T
            queries = query_ref[0, at, :]
            dout = dout_ref[at, :]
            weighted = jnp.sum(
                dout.astype(F32) * out_ref[at, :].astype(F32), axis=0, keepdims=True
            )
            totals = total_ref[0, head : head + 1, :]
            dquery = jnp.zeros((HEAD, span), F32)
            for start in range(0, live, key_block):
                rows = slice(start, start + key_block)
                probs = jnp.exp2(dot(keys[rows], queries, NN) * LOG2_SCALE - totals)
                dprobs = dot(values[rows], dout, NN)
                dscores = (probs * (dprobs - weighted)).astype(BF)
                dvalue = dot(dout, probs.astype(BF), NT)
                dkey = dot(queries, dscores, NT) * HEAD ** (-0.5)
                dquery = dquery + dot(key_ref[0, at, rows], dscores, NN)
                turned(dkey, cos_ref[:, rows], sin_ref[:, rows], grad_ref, 1, head, rows)
                grad_ref[2, at, rows] = dvalue.astype(BF)
            turned(dquery * HEAD ** (-0.5), cos_ref[...], sin_ref[...], grad_ref, 0, head, slice(0, span))
        if live < span:
            empty = jnp.zeros((per_step * HEAD, span - live), BF)
            grad_ref[1, :, live:] = empty
            grad_ref[2, :, live:] = empty

    def body(length_ref, *refs):
        for live in live_lengths(span):

            @pl.when(length_ref[0] == live)
            def _():
                one_length(live, *refs)

    rows = per_step * HEAD

    def part(c):
        return pl.BlockSpec((1, rows, span), lambda i, n: (c, i, 0))

    flat = pl.BlockSpec((rows, span), lambda i, n: (i, 0))
    table = pl.BlockSpec((HALF, span), lambda i, n: (0, 0))
    return call(
        body,
        (width // rows,),
        [part(0), part(1), part(2), flat, flat, pl.BlockSpec((1, per_step, span), lambda i, n: (i, 0, 0)), table, table],
        [pl.BlockSpec((3, rows, span), lambda i, n: (0, i, 0))],
        [shaped((3, width, span), BF)],
        40 * span * span * width,
        prefetch=1,
    )(length, joined, joined, joined, attended, dattended, totals, cosine, sine)[0]


def middle_forward(attended, tokens, outs, ups, biases, vectors):
    width, span = attended[0].shape
    features = tokens.shape[1]
    hidden = ups[0].shape[1]
    rows = 256

    def body(att_a, att_b, tok_ref, out_a, out_b, up_a, up_b, bias_a, bias_b, vec_ref, branch_ref, h_ref, act_a, act_b, slope_a, slope_b):
        branch = dot(att_a[...], out_a[...], TN) + dot(att_b[...], out_b[...], TN)
        branch_ref[...] = branch
        middle = tok_ref[...].astype(F32) + vec_ref[0:1, :] * branch
        hat, _ = normed_rows(middle)
        h = (hat * vec_ref[1:2, :] + vec_ref[2:3, :]).astype(BF)
        h_ref[...] = h
        for up, bias, act, slope in ((up_a, bias_a, act_a, slope_a), (up_b, bias_b, act_b, slope_b)):
            for at in range(0, hidden, 256):
                columns = slice(at, at + 256)
                upper = dot(h, up[:, columns], NN) + bias[0:1, columns]
                square = upper * upper
                tanh = jnp.tanh(upper * (GELU_A + (GELU_A * GELU_B) * square))
                half = 0.5 * upper
                act[:, columns] = (half + half * tanh).astype(BF)
                slope[:, columns] = (
                    (0.5 + 0.5 * tanh)
                    + half * (1.0 - tanh * tanh) * (GELU_A + (3.0 * GELU_A * GELU_B) * square)
                ).astype(BF)

    whole = lambda i: (0, 0)
    att = pl.BlockSpec((width, rows), lambda i: (0, i))
    tok = pl.BlockSpec((rows, features), lambda i: (i, 0))
    wide = pl.BlockSpec((rows, hidden), lambda i: (i, 0))
    fixed = lambda a: pl.BlockSpec(a.shape, whole)
    return call(
        body,
        (span // rows,),
        [att, att, tok] + [fixed(a) for a in (*outs, *ups, *biases, vectors)],
        [tok, tok, wide, wide, wide, wide],
        [shaped((span, features), F32), shaped((span, features), BF)] + [shaped((span, hidden), BF)] * 4,
        4 * span * features * (width + hidden),
    )(*attended, tokens, *outs, *ups, *biases, vectors)


def hidden_back(act, slope, down, dbranch, h, out_type):
    span, hidden = act.shape
    features = h.shape[1]
    block = 256
    per = features // block

    def body(act_ref, slope_ref, down_ref, db_ref, h_ref, du_ref, gd_ref, gu_ref, gb_ref):
        gd_ref[...] = dot(act_ref[...], db_ref[...], TN).astype(out_type)
        du = (dot(db_ref[...], down_ref[...], NT) * slope_ref[...].astype(F32)).astype(BF)
        du_ref[...] = du
        gb_ref[...] = jnp.sum(du.astype(F32), axis=0, keepdims=True)
        gu_ref[0] = dot(h_ref[...], du, TN).astype(out_type)

    whole = lambda i: (0, 0)
    column = pl.BlockSpec((span, block), lambda i: (0, i))
    fixed = pl.BlockSpec((span, features), whole)
    return call(
        body,
        (hidden // block,),
        [column, column, pl.BlockSpec((block, features), lambda i: (i, 0)), fixed, fixed],
        [
            column,
            pl.BlockSpec((block, features), lambda i: (i, 0)),
            pl.BlockSpec((1, features, block), lambda i: (i // per, 0, i % per)),
            pl.BlockSpec((1, block), lambda i: (0, i)),
        ],
        [
            shaped((span, hidden), BF),
            shaped((hidden, features), out_type),
            shaped((hidden // features, features, features), out_type),
            shaped((1, hidden), F32),
        ],
        6 * span * features * hidden,
    )(act, slope, down, dbranch, h)


def middle_back(dupper, ups, outs, branch, tokens, upstream, vectors):
    span, hidden = dupper[0].shape
    features = tokens.shape[1]
    width = outs[0].shape[0]
    rows = 256

    def body(du_a, du_b, up_a, up_b, out_a, out_b, branch_ref, tok_ref, g_ref, vec_ref, dmid_ref, db_ref, da_a, da_b, sum_ref):
        dh = dot(du_a[...], up_a[...], NT) + dot(du_b[...], up_b[...], NT)
        branch = branch_ref[...]
        hat, inverse = normed_rows(tok_ref[...].astype(F32) + vec_ref[0:1, :] * branch)
        dhat = dh * hat
        e = dh * vec_ref[1:2, :]
        e_mean = jnp.mean(e, axis=-1, keepdims=True)
        eh_mean = jnp.mean(e * hat, axis=-1, keepdims=True)
        dmid = g_ref[...].astype(F32) + (e - e_mean - hat * eh_mean) * inverse
        dmid_ref[...] = dmid
        db = (vec_ref[0:1, :] * dmid).astype(BF)
        db_ref[...] = db
        da_a[...] = dot(out_a[...], db, NT).astype(BF)
        da_b[...] = dot(out_b[...], db, NT).astype(BF)
        sums = jnp.concatenate(
            [
                jnp.sum(dh, axis=0, keepdims=True),
                jnp.sum(dhat, axis=0, keepdims=True),
                jnp.sum(dmid * branch, axis=0, keepdims=True),
                jnp.zeros((5, features), F32),
            ],
            axis=0,
        )

        @pl.when(pl.program_id(0) == 0)
        def _():
            sum_ref[...] = sums

        @pl.when(pl.program_id(0) > 0)
        def _():
            sum_ref[...] += sums

    whole = lambda i: (0, 0)
    tok = pl.BlockSpec((rows, features), lambda i: (i, 0))
    wide = pl.BlockSpec((rows, hidden), lambda i: (i, 0))
    att = pl.BlockSpec((width, rows), lambda i: (0, i))
    fixed = lambda a: pl.BlockSpec(a.shape, whole)
    return call(
        body,
        (span // rows,),
        [wide, wide] + [fixed(a) for a in (*ups, *outs)] + [tok, tok, tok, fixed(vectors)],
        [tok, tok, att, att, pl.BlockSpec((8, features), whole)],
        [
            shaped((span, features), F32),
            shaped((span, features), BF),
            shaped((width, span), BF),
            shaped((width, span), BF),
            shaped((8, features), F32),
        ],
        4 * span * features * (width + hidden),
    )(*dupper, *ups, *outs, branch, tokens, upstream, vectors)


def finish_forward(acts, downs, branch, tokens, upstream, vectors):
    span, hidden = acts[0].shape
    features = tokens.shape[1]
    rows = 256

    def body(act_a, act_b, down_a, down_b, branch_ref, tok_ref, g_ref, vec_ref, out_ref, sum_ref):
        second = dot(act_a[...], down_a[...], NN) + dot(act_b[...], down_b[...], NN) + vec_ref[2:3, :]
        middle = tok_ref[...].astype(F32) + vec_ref[0:1, :] * branch_ref[...]
        out_ref[...] = (middle + vec_ref[1:2, :] * second).astype(BF)
        sums = jnp.sum(g_ref[...].astype(F32) * second, axis=0, keepdims=True)

        @pl.when(pl.program_id(0) == 0)
        def _():
            sum_ref[...] = sums

        @pl.when(pl.program_id(0) > 0)
        def _():
            sum_ref[...] += sums

    whole = lambda i: (0, 0)
    tok = pl.BlockSpec((rows, features), lambda i: (i, 0))
    wide = pl.BlockSpec((rows, hidden), lambda i: (i, 0))
    fixed = lambda a: pl.BlockSpec(a.shape, whole)
    return call(
        body,
        (span // rows,),
        [wide, wide] + [fixed(a) for a in downs] + [tok, tok, tok, fixed(vectors)],
        [tok, pl.BlockSpec((1, features), whole)],
        [shaped((span, features), BF), shaped((1, features), F32)],
        4 * span * features * hidden,
    )(*acts, *downs, branch, tokens, upstream, vectors)


def project_weight_back(h, djoined, out_type):
    span, features = h.shape
    _, width, _ = djoined.shape

    def body(h_ref, dj_ref, out_ref):
        out_ref[0] = dot(h_ref[...], dj_ref[0], TT).astype(out_type)

    return call(
        body,
        (3,),
        [
            pl.BlockSpec((span, features), lambda c: (0, 0)),
            pl.BlockSpec((1, width, span), lambda c: (c, 0, 0)),
        ],
        [pl.BlockSpec((1, features, width), lambda c: (c, 0, 0))],
        [shaped((3, features, width), out_type)],
        6 * span * features * width,
    )(h, djoined)[0]


def project_back(djoined, weights, tokens, dmiddle, vectors):
    _, width, span = djoined[0].shape
    features = tokens.shape[1]
    rows = 256

    def body(dj_a, dj_b, w_a, w_b, tok_ref, dmid_ref, vec_ref, out_ref, sum_ref):
        dh = jnp.zeros((rows, features), F32)
        for c in range(3):
            dh = dh + dot(dj_a[c], w_a[c], TT) + dot(dj_b[c], w_b[c], TT)
        hat, inverse = normed_rows(tok_ref[...].astype(F32))
        e = dh * vec_ref[0:1, :]
        e_mean = jnp.mean(e, axis=-1, keepdims=True)
        eh_mean = jnp.mean(e * hat, axis=-1, keepdims=True)
        out_ref[...] = dmid_ref[...] + (e - e_mean - hat * eh_mean) * inverse
        sums = jnp.concatenate(
            [
                jnp.sum(dh, axis=0, keepdims=True),
                jnp.sum(dh * hat, axis=0, keepdims=True),
                jnp.zeros((6, features), F32),
            ],
            axis=0,
        )

        @pl.when(pl.program_id(0) == 0)
        def _():
            sum_ref[...] = sums

        @pl.when(pl.program_id(0) > 0)
        def _():
            sum_ref[...] += sums

    whole = lambda i: (0, 0)
    tok = pl.BlockSpec((rows, features), lambda i: (i, 0))
    joined = pl.BlockSpec((3, width, rows), lambda i: (0, 0, i))
    weight = pl.BlockSpec((3, features, width), lambda i: (0, 0, 0))
    return call(
        body,
        (span // rows,),
        [joined, joined, weight, weight, tok, tok, pl.BlockSpec(vectors.shape, whole)],
        [tok, pl.BlockSpec((8, features), whole)],
        [shaped((span, features), F32), shaped((8, features), F32)],
        12 * span * features * width,
    )(*djoined, *weights, tokens, dmiddle, vectors)


def halving_steps(size):
    if size == 16:
        return [
            (1, lambda d: d & 1),
            (2, lambda d: (d >> 1) & 1),
            (4, lambda d: ((d >> 2) ^ (d >> 3)) & 1),
            (12, lambda d: (d >> 3) & 1),
        ]
    steps, mask = [], 1
    while mask < size:
        steps.append((mask, partial(lambda shift, d: (d >> shift) & 1, len(steps))))
        mask *= 2
    return steps


def sum_over_dp(total, dp_size, tensor_size, dp_index, tensor_index, orders):
    if dp_size & (dp_size - 1) or total.shape[0] % dp_size:
        return lax.psum(total, "dp")
    steps = halving_steps(dp_size)
    count = len(steps)
    rounds = []
    for at in range(count):
        chosen = [steps[orders[t % len(orders)][at] if count == 4 else (at + t) % count] for t in range(tensor_size)]
        pairs = [
            (d * tensor_size + t, (d ^ chosen[t][0]) * tensor_size + t)
            for d in range(dp_size)
            for t in range(tensor_size)
        ]
        bit = chosen[0][1](dp_index)
        for t in range(1, tensor_size):
            bit = jnp.where(tensor_index == t, chosen[t][1](dp_index), bit)
        rounds.append((pairs, bit))
    for pairs, bit in rounds:
        half = total.shape[0] // 2
        leaving = lax.dynamic_slice_in_dim(total, (1 - bit) * half, half, 0).astype(BF)
        arrived = lax.ppermute(leaving, ("dp", "tensor"), pairs)
        total = lax.dynamic_slice_in_dim(total, bit * half, half, 0) + arrived.astype(F32)
    total = total.astype(BF)
    for pairs, bit in rounds[::-1]:
        half = total.shape[0]
        arrived = lax.ppermute(total, ("dp", "tensor"), pairs)
        both = jnp.zeros((2 * half,) + total.shape[1:], BF)
        both = lax.dynamic_update_slice_in_dim(both, total, bit * half, 0)
        total = lax.dynamic_update_slice_in_dim(both, arrived, (1 - bit) * half, 0)
    return total.astype(F32)


def per_device(
    dp_size,
    tensor_size,
    tokens,
    condition,
    lengths,
    modulation_weight,
    modulation_bias,
    first_gain,
    query_key_value_weight,
    attention_out_weight,
    second_gain,
    up_projection_weight,
    upward_bias,
    down_projection_weight,
    downward_bias,
    cotangent,
):
    sequences, span, features = tokens.shape
    hidden = up_projection_weight.shape[1]
    width = attention_out_weight.shape[0]
    dp_index = lax.axis_index("dp")
    mine = lax.axis_index("tensor")
    swap = [(0, 1), (1, 0)]

    def from_sibling(value):
        return lax.ppermute(value, "tensor", swap)

    def ordered(own, other, axis):
        return jnp.where(
            mine == 0,
            jnp.concatenate([own, other], axis=axis),
            jnp.concatenate([other, own], axis=axis),
        )

    qkv_own = query_key_value_weight.transpose(1, 0, 2)
    qkv_weights = (qkv_own, from_sibling(qkv_own))
    out_weights = (attention_out_weight, from_sibling(attention_out_weight))
    up_weights = (up_projection_weight, from_sibling(up_projection_weight))
    up_biases = (upward_bias[None], from_sibling(upward_bias)[None])
    down_weights = (down_projection_weight, from_sibling(down_projection_weight))
    gone = lax.dynamic_index_in_dim(cotangent, 1 - mine, 0, keepdims=False)
    kept = lax.dynamic_index_in_dim(cotangent, mine, 0, keepdims=False)
    upstream = ordered(kept, from_sibling(gone), 0)
    rows = lax.dynamic_index_in_dim(tokens, mine, 0, keepdims=False)
    length = lax.dynamic_slice_in_dim(lengths, mine, 1, 0)

    cond_float = condition.astype(F32)
    silu_values, silu_pull = jax.vjp(jax.nn.silu, cond_float)
    silu_cond = silu_values.astype(BF)
    mods = dot(silu_cond, modulation_weight, NN) + modulation_bias
    mods = lax.dynamic_index_in_dim(mods, mine, 0, keepdims=False).reshape(6, features)
    shift_one, scale_one, gate_one, shift_two, scale_two, gate_two = mods
    empty = jnp.zeros((features,), F32)
    gain_one = first_gain * (1.0 + scale_one)
    gain_two = second_gain * (1.0 + scale_two)
    vectors_one = jnp.stack([gain_one, shift_one] + [empty] * 6)
    vectors_two = jnp.stack([gate_one, gain_two, shift_two] + [empty] * 5)
    vectors_three = jnp.stack([gate_one, gate_two, downward_bias] + [empty] * 5)
    cosine, sine = (jnp.asarray(table) for table in rotary_tables(span))

    leading, joined_own = project(rows, qkv_weights[0], vectors_one, cosine, sine, True)
    (joined_other,) = project(leading, qkv_weights[1], vectors_one, cosine, sine, False)
    attended_own, totals_own = attend(length, joined_own)
    attended_other, totals_other = attend(length, joined_other)
    attended = (attended_own, attended_other)
    branch_one, trailing, act_own, act_other, slope_own, slope_other = middle_forward(
        attended, rows, out_weights, up_weights, up_biases, vectors_two
    )
    dbranch = (gate_two * upstream.astype(F32)).astype(BF)
    grad_downward_bias = jnp.sum(dbranch, axis=0, dtype=F32)
    dupper_other, gd_other, gu_other, gb_other = hidden_back(
        act_other, slope_other, down_weights[1], dbranch, trailing, BF
    )
    gd_other = from_sibling(gd_other)
    gu_other = from_sibling(gu_other)
    dupper_own, gd_own, gu_own, gb_own = hidden_back(
        act_own, slope_own, down_weights[0], dbranch, trailing, F32
    )
    grad_upward_bias = ordered(gb_own, gb_other, 1)

    def reduced(total, orders):
        return sum_over_dp(total, dp_size, tensor_size, dp_index, mine, orders)

    grad_downward_weight = reduced(gd_own + gd_other.astype(F32), ((0, 1, 2, 3), (1, 0, 3, 2)))
    grad_upward_weight = reduced(
        (gu_own + gu_other.astype(F32)).reshape(hidden, features), ((2, 3, 0, 1), (3, 2, 1, 0))
    )
    grad_upward_weight = (
        grad_upward_weight.reshape(hidden // features, features, features)
        .transpose(1, 0, 2)
        .reshape(features, hidden)
    )
    dmiddle, dbranch_one, dattended_own, dattended_other, sums_two = middle_back(
        (dupper_own, dupper_other), up_weights, out_weights, branch_one, rows, upstream, vectors_two
    )
    go_other = from_sibling(dot(attended_other, dbranch_one, NN).astype(BF))
    go_own = dot(attended_own, dbranch_one, NN) + go_other.astype(F32)
    grad_output_weight = reduced(go_own, ((0, 1, 2, 3), (1, 0, 3, 2)))

    djoined_other = attend_back(
        length, joined_other, attended_other, dattended_other, totals_other, cosine, sine
    )
    gq_other = from_sibling(project_weight_back(leading, djoined_other, BF))
    djoined_own = attend_back(
        length, joined_own, attended_own, dattended_own, totals_own, cosine, sine
    )
    gq_own = project_weight_back(leading, djoined_own, F32)
    grad_input_weight = reduced(
        (gq_own + gq_other.astype(F32)).reshape(3 * features, width), ((0, 1, 2, 3), (1, 0, 3, 2))
    )
    grad_input_weight = grad_input_weight.reshape(3, features, width).transpose(1, 0, 2)

    output, dgate_two = finish_forward(
        (act_own, act_other), down_weights, branch_one, rows, upstream, vectors_three
    )
    grad_rows, sums_one = project_back(
        (djoined_own, djoined_other), qkv_weights, rows, dmiddle, vectors_one
    )

    def by_halves(value):
        halves = value.reshape(2, span // 2, features)
        kept = lax.dynamic_index_in_dim(halves, mine, 0, keepdims=True)
        gone = lax.dynamic_index_in_dim(halves, 1 - mine, 0, keepdims=True)
        return ordered(kept, from_sibling(gone), 0)

    output = by_halves(output)
    grad_tokens = by_halves(grad_rows)

    small = jnp.concatenate(
        [
            sums_one[0:1],
            sums_one[1:2] * first_gain,
            sums_two[2:3],
            sums_two[0:1],
            sums_two[1:2] * second_gain,
            dgate_two,
            sums_one[1:2] * (1.0 + scale_one),
            sums_two[1:2] * (1.0 + scale_two),
            grad_downward_bias[None],
            grad_upward_bias.reshape(-1, features),
        ],
        axis=0,
    )
    gathered = lax.all_gather(small, ("dp", "tensor"), axis=0)
    everyone = lax.all_gather(silu_cond, "dp", axis=0, tiled=True)
    dmods_low = gathered[:, :6].reshape(-1, 6 * features).astype(BF)
    grad_modulation_bias = jnp.sum(dmods_low, axis=0, dtype=F32)
    grad_modulation_weight = dot(everyone, dmods_low, TN)
    pair = lax.dynamic_slice_in_dim(dmods_low, dp_index * sequences, sequences, 0)
    grad_condition = silu_pull(dot(pair, modulation_weight, NT))[0]
    sums = jnp.sum(gathered[:, 6:], axis=0)
    grad_upward_bias = lax.dynamic_slice_in_dim(sums[3:].reshape(-1), mine * hidden, hidden, 0)
    return (
        output,
        grad_tokens,
        grad_condition,
        grad_modulation_weight,
        grad_modulation_bias,
        sums[0],
        grad_input_weight,
        grad_output_weight,
        sums[1],
        grad_upward_weight,
        grad_upward_bias,
        grad_downward_weight,
        sums[2],
    )


def solution(mesh):
    placed = (
        P("dp", None, None),
        P("dp", None),
        P("dp"),
        P(),
        P(),
        P(),
        P(None, None, "tensor"),
        P("tensor", None),
        P(),
        P(None, "tensor"),
        P("tensor"),
        P("tensor", None),
        P(),
        P("dp", "tensor", None),
    )
    return jax.shard_map(
        partial(per_device, mesh.shape["dp"], mesh.shape["tensor"]),
        mesh=mesh,
        in_specs=placed,
        out_specs=(
            P("dp", "tensor", None),
            P("dp", "tensor", None),
            P("dp", None),
            P(),
            P(),
            P(),
            P(None, None, "tensor"),
            P("tensor", None),
            P(),
            P(None, "tensor"),
            P("tensor"),
            P("tensor", None),
            P(),
        ),
        check_vma=False,
    )
```

time: 971 us -> 472 us (0.49)
  waiting for transfers between devices: 427 us -> 106 us
  matrix products: 206 us -> 6.09 us
  Pallas kernels: 0 us -> 172 us
  local copies, waits for them, and re-layouts: 123 us -> 24.9 us
  other arithmetic: 104 us -> 32.8 us
  starting transfers between devices: 0.91 us -> 64.7 us
  blocking collectives: 85.6 us -> 40.3 us
    psum x1 -> x0, waiting for transfers between devices: 374 us -> none  [per_device(): lax.psum((grad_modulation_weight, grad_modulation_bias, grad_first_gain,...]
    dot_general x43 -> x5, matrix products: 206 us -> 6.09 us  [the longest x1 2.18 us: per_device(): go_other = from_sibling(dot(attended_other, dbranch_one, NN).astype(BF))]
    pallas_call x0 -> x14, Pallas kernels: none -> 172 us  [the longest x2 36.4 us: attend_back(): call(body, (width // rows,), [part(0), part(1), part(2), flat, flat, pl.B...]
    psum x2 -> x0, blocking collectives: 85.6 us -> none  [the longest x1 82 us: per_device(): lax.psum((grad_modulation_weight, grad_modulation_bias, grad_first_gain,...]
    ppermute x0 -> x44, waiting for transfers between devices: none -> 83.6 us  [the longest x16 45.2 us: sum_over_dp(): arrived = lax.ppermute(total, ('dp', 'tensor'), pairs)]
    ppermute x0 -> x44, starting transfers between devices: none -> 64.6 us  [the longest x16 39.1 us: sum_over_dp(): arrived = lax.ppermute(total, ('dp', 'tensor'), pairs)]
    all_gather x0 -> x1, blocking collectives: none -> 40.3 us  [per_device(): everyone = lax.all_gather(silu_cond, 'dp', axis=0, tiled=True)]
    reduce_sum x15 -> x3, other arithmetic: 44 us -> 5.26 us  [the longest x1 3.93 us: per_device(): grad_downward_bias = jnp.sum(dbranch, axis=0, dtype=F32)]
  transfers between devices with their start and end apart: 8 -> 45, of which waited for: 7 -> 19; matrix products, arithmetic and copies ran while one was open for 7% -> 13% of each run, Pallas kernels for 0% -> 34%
where the time goes in v1:
time: 472 us; the launch traced here: 463 us
  Pallas kernels  172 us (36%)
  waiting for transfers between devices  106 us (22%)
  starting transfers between devices  64.7 us (14%)
  blocking collectives  40.3 us (9%)
  other arithmetic  32.8 us (7%)
  local copies, waits for them, and re-layouts  24.9 us (5%)
  between operations  15.5 us (3%)
  matrix products  6.09 us (1%)
    ppermute x16, waiting for transfers between devices, sum_over_dp(): arrived = lax.ppermute(total, ('dp', 'tensor'), pairs)  45.2 us
    all_gather x1, blocking collectives, per_device(): everyone = lax.all_gather(silu_cond, 'dp', axis=0, tiled=True)  40.3 us
    ppermute x16, starting transfers between devices, sum_over_dp(): arrived = lax.ppermute(total, ('dp', 'tensor'), pairs)  39.1 us
    ppermute x16, waiting for transfers between devices, sum_over_dp(): arrived = lax.ppermute(leaving, ('dp', 'tensor'), pairs)  38.3 us
    pallas_call x2, Pallas kernels, attend_back(): call(body, (width // rows,), [part(0), part(1), part(2), flat, flat, pl.B...  36.4 us
    pallas_call x2, Pallas kernels, hidden_back(): call(body, (hidden // block,), [column, column, pl.BlockSpec((block, feat...  29.8 us
    all_gather x1, waiting for transfers between devices, per_device(): gathered = lax.all_gather(small, ('dp', 'tensor'), axis=0)  22.8 us
    pallas_call x2, Pallas kernels, attend(): call(body, (width // rows,), [part(0), part(1), part(2)], [pl.BlockSpec((...  21.7 us
  transfers between devices with their start and end apart: 45, of which 19 were waited for; matrix products, arithmetic and copies ran while one was open for 13% of the time, Pallas kernels for 34%

profile of v1, /device:TPU:0, one launch (start us, length us, event | category | flops | bytes accessed | tf_op | source)
XLA Modules:
  0.0 463.1 jit_solution(13670979070916796914)
XLA Ops:
  14.5 7.5 %shard_map.255 = (bf16[1024,768]{1,0:T(8,128)(2,1)}, bf16[3,384,1024]{2,1,0:T(8,128)(2,1)}) custom-call(bf16[1024,768]{1,0:T(8,128)(2,1)} %dynamic-slice_bitcast_fusion.source_ref.tok_ref, bf16[3,768,384]{2,1,0:T(8,128)(2,1)} %bitcast.54, f32[8,768]{1,0:T(8,128)} %pad_maximum_fusion.vector_ref.vec_ref, f32[32,1024]{1,0:T(8,128)} %constant.53.clone.cos_ref.refs_6_, ...), custom_call_target="tpu_custom_call" | custom-call | flops 1811939328 | bytes 7864320 | tf_op jit(solution)/shard_map/pallas_call | solution.py:107
  22.0 10.9 %shard_map.256 = (bf16[384,1024]{1,0:T(8,128)(2,1)}, f32[3,2,1024]{2,1,0:T(2,128)}) custom-call(s32[1]{0:T(128)} %dynamic_slice.134.length_ref, bf16[3,384,1024]{2,1,0:T(8,128)(2,1)} %get-tuple-element.42.query_ref.key_ref.value_ref.refs_0_.refs_1_.refs_2_, bf16[3,384,1024]{2,1,0:T(8,128)(2,1)} %get-tuple-element.42.query_ref.key_ref.value_ref.refs_0_.refs_1_.refs_2_, ...), custom_call_target="tpu_custom_call" | custom-call | flops 6442450944 | bytes 1622016 | tf_op jit(solution)/shard_map/pallas_call | solution.py:181
  34.2 4.3 collective-permute-start.1
  39.1 3.9 convert_reduce_fusion
  43.0 6.1 %shard_map.257.query_ref.key_ref.value_ref.refs_0_.refs_1_.refs_2_ = bf16[3,384,1024]{2,1,0:T(8,128)(2,1)} custom-call(bf16[1024,768]{1,0:T(8,128)(2,1)} %get-tuple-element.44.source_ref.h_ref, bf16[3,768,384]{2,1,0:T(8,128)(2,1)} %collective-permute-done.weight_ref.w_b, f32[8,768]{1,0:T(8,128)} %pad_maximum_fusion.vector_ref.vec_ref, ...), custom_call_target="tpu_custom_call" | custom-call | flops 1811939328 | bytes 4718592 | tf_op jit(solution)/shard_map/pallas_call | solution.py:107
  49.1 10.8 %shard_map.258 = (bf16[384,1024]{1,0:T(8,128)(2,1)}, f32[3,2,1024]{2,1,0:T(2,128)}) custom-call(s32[1]{0:T(128)} %dynamic_slice.134.length_ref, bf16[3,384,1024]{2,1,0:T(8,128)(2,1)} %shard_map.257.query_ref.key_ref.value_ref.refs_0_.refs_1_.refs_2_, bf16[3,384,1024]{2,1,0:T(8,128)(2,1)} %shard_map.257.query_ref.key_ref.value_ref.refs_0_.refs_1_.refs_2_, ...), custom_call_target="tpu_custom_call" | custom-call | flops 6442450944 | bytes 1622016 | tf_op jit(solution)/shard_map/pallas_call | solution.py:181
  60.7 20.4 %shard_map.259 = (f32[1024,768]{1,0:T(8,128)}, bf16[1024,768]{1,0:T(8,128)(2,1)}, bf16[1024,1536]{1,0:T(8,128)(2,1)}, bf16[1024,1536]{1,0:T(8,128)(2,1)}, bf16[1...) custom-call(bf16[384,1024]{1,0:T(8,128)(2,1)} %get-tuple-element.43.att_a.refs_3_, ...), custom_call_target="tpu_custom_call" | custom-call | flops 6039797760 | bytes 34603008 | tf_op jit(solution)/shard_map/pallas_call | solution.py:291
  81.1 14.8 %shard_map.262 = (bf16[1024,1536]{1,0:T(8,128)(2,1)}, bf16[1536,768]{1,0:T(8,128)(2,1)}, bf16[2,768,768]{2,1,0:T(8,128)(2,1)}, f32[1,1536]{1,0:T(1,128)}) custom-call(bf16[1024,1536]{1,0:T(8,128)(2,1)} %get-tuple-element.47.act_b.act_ref, bf16[1024,1536]{1,0:T(8,128)(2,1)} %get-tuple-element.53.slope_ref, ...), custom_call_target="tpu_custom_call" | custom-call | flops 7247757312 | bytes 15740928 | tf_op jit(solution)/shard_map/pallas_call | solution.py:317
  96.0 4.2 collective-permute-start.35
  100.2 14.9 %shard_map.261 = (bf16[1024,1536]{1,0:T(8,128)(2,1)}, f32[1536,768]{1,0:T(8,128)}, f32[2,768,768]{2,1,0:T(8,128)}, f32[1,1536]{1,0:T(1,128)}) custom-call(bf16[1024,1536]{1,0:T(8,128)(2,1)} %get-tuple-element.46.act_a.act_ref, bf16[1024,1536]{1,0:T(8,128)(2,1)} %get-tuple-element.50.slope_ref, bf16[1536,768]{1,0:T(8,128)(2,1)} %down_ref.1, ...), custom_call_target="tpu_custom_call" | custom-call | flops 7247757312 | bytes 25178112 | tf_op jit(solution)/shard_map/pallas_call | solution.py:317
  115.1 16.3 %shard_map.263 = (f32[1024,768]{1,0:T(8,128)}, bf16[1024,768]{1,0:T(8,128)(2,1)}, bf16[384,1024]{1,0:T(8,128)(2,1)}, bf16[384,1024]{1,0:T(8,128)(2,1)}, f32[8,768]{1,0:T(8,128)}) custom-call(bf16[1024,1536]{1,0:T(8,128)(2,1)} %get-tuple-element.52.du_a, bf16[1024,1536]{1,0:T(8,128)(2,1)} %get-tuple-element.54.du_b, bf16[768,1536]{1,0:T(8,128)(2,1)} %up_a.3, ...), custom_call_target="tpu_custom_call" | custom-call | flops 6039797760 | bytes 12632064 | tf_op jit(solution)/shard_map/pallas_call | solution.py:380
  133.7 18.1 %shard_map.265.dj_b.dj_ref = bf16[3,384,1024]{2,1,0:T(8,128)(2,1)} custom-call(s32[1]{0:T(128)} %dynamic_slice.134.length_ref, bf16[3,384,1024]{2,1,0:T(8,128)(2,1)} %shard_map.257.query_ref.key_ref.value_ref.refs_0_.refs_1_.refs_2_, bf16[3,384,1024]{2,1,0:T(8,128)(2,1)} %shard_map.257.query_ref.key_ref.value_ref.refs_0_.refs_1_.refs_2_, ...), custom_call_target="tpu_custom_call" | custom-call | flops 16106127360 | bytes 4718592 | tf_op jit(solution)/shard_map/pallas_call | solution.py:249
  151.9 5.8 %shard_map.268 = bf16[3,768,384]{2,1,0:T(8,128)(2,1)} custom-call(bf16[1024,768]{1,0:T(8,128)(2,1)} %get-tuple-element.44.source_ref.h_ref, bf16[3,384,1024]{2,1,0:T(8,128)(2,1)} %shard_map.265.dj_b.dj_ref), custom_call_target="tpu_custom_call" | custom-call | flops 1811939328 | bytes 3538944 | tf_op jit(solution)/shard_map/pallas_call | solution.py:436
  158.2 18.2 %shard_map.264.dj_a.dj_ref = bf16[3,384,1024]{2,1,0:T(8,128)(2,1)} custom-call(s32[1]{0:T(128)} %dynamic_slice.134.length_ref, bf16[3,384,1024]{2,1,0:T(8,128)(2,1)} %get-tuple-element.42.query_ref.key_ref.value_ref.refs_0_.refs_1_.refs_2_, bf16[3,384,1024]{2,1,0:T(8,128)(2,1)} %get-tuple-element.42.query_ref.key_ref.value_ref.refs_0_.refs_1_.refs_2_, ...), custom_call_target="tpu_custom_call" | custom-call | flops 16106127360 | bytes 4718592 | tf_op jit(solution)/shard_map/pallas_call | solution.py:249
  176.4 11.1 %shard_map.266 = (f32[1024,768]{1,0:T(8,128)}, f32[8,768]{1,0:T(8,128)}) custom-call(bf16[3,384,1024]{2,1,0:T(8,128)(2,1)} %shard_map.264.dj_a.dj_ref, bf16[3,384,1024]{2,1,0:T(8,128)(2,1)} %shard_map.265.dj_b.dj_ref, bf16[3,768,384]{2,1,0:T(8,128)(2,1)} %bitcast.55, bf16[3,768,384]{2,1,0:T(8,128)(2,1)} %collective-permute-done.weight_ref.w_b, ...), custom_call_target="tpu_custom_call" | custom-call | flops 3623878656 | bytes 6340608 | tf_op jit(solution)/shard_map/pallas_call | solution.py:484
  198.8 10.9 %shard_map.260 = (bf16[1024,768]{1,0:T(8,128)(2,1)}, f32[1,768]{1,0:T(1,128)}) custom-call(bf16[1024,1536]{1,0:T(8,128)(2,1)} %get-tuple-element.46.act_a.act_ref, bf16[1024,1536]{1,0:T(8,128)(2,1)} %get-tuple-element.47.act_b.act_ref, bf16[1536,768]{1,0:T(8,128)(2,1)} %down_ref.1, bf16[1536,768]{1,0:T(8,128)(2,1)} %collective-permute-done.4.down_b.down_ref, ...), custom_call_target="tpu_custom_call" | custom-call | flops 4831838208 | bytes 3151872 | tf_op jit(solution)/shard_map/pallas_call | solution.py:419
  214.8 40.3 %all-gather.2 = bf16[16,2,128]{2,1,0:T(2,128)(2,1)S(1)} all-gather(bf16[1,2,128]{2,1,0:T(2,128)(2,1)S(1)} %fusion.11), channel_id=1, replica_groups=mesh['dp'=16,'tensor'=2] {'dp'}, dimensions={0}, use_global_device_ids=true | all-gather | bytes 8704 | tf_op jit(solution)/shard_map/all_gather | solution.py:686
  255.2 6.5 %shard_map.267 = f32[3,768,384]{2,1,0:T(8,128)} custom-call(bf16[1024,768]{1,0:T(8,128)(2,1)} %get-tuple-element.44.source_ref.h_ref, bf16[3,384,1024]{2,1,0:T(8,128)(2,1)} %shard_map.264.dj_a.dj_ref), custom_call_target="tpu_custom_call" | custom-call | flops 1811939328 | bytes 7077888 | tf_op jit(solution)/shard_map/pallas_call | solution.py:436
  263.2 4.3 collective-permute-done.23
  273.0 4.0 maximum_select_fusion
  291.0 6.7 %collective-permute-done.9 = bf16[1152,384]{1,0:T(8,128)(2,1)S(1)} collective-permute-done((bf16[1152,384]{1,0:T(8,128)(2,1)S(1)}, bf16[1152,384]{1,0:T(8,128)(2,1)S(1)}, u32[]{:S(2)}, u32[]{:S(2)}) %collective-permute-start.9) | collective-permute-done | bytes 884768 | tf_op jit(solution)/shard_map/ppermute | solution.py:529
  298.1 22.8 %all-gather.5.cloned.1.call-done = f32[32,13,768]{2,1,0:T(8,128)} async-done(((f32[1,13,768]{2,1,0:T(8,128)}), f32[32,13,768]{2,1,0:T(8,128)}) %all-gather.5.cloned.1.call-update) | async-done | bytes 1277968 | tf_op jit(solution)/shard_map/all_gather | solution.py:685
  327.9 5.3 %collective-permute-done.11 = bf16[288,384]{1,0:T(8,128)(2,1)S(1)} collective-permute-done((bf16[288,384]{1,0:T(8,128)(2,1)S(1)}, bf16[288,384]{1,0:T(8,128)(2,1)S(1)}, u32[]{:S(2)}, u32[]{:S(2)}) %collective-permute-start.11) | collective-permute-done | bytes 221216 | tf_op jit(solution)/shard_map/ppermute | solution.py:529
  336.5 3.7 collective-permute-done.12
  351.7 3.7 collective-permute-done.14
  356.3 11.8 %collective-permute-done.28 = bf16[384,768]{1,0:T(8,128)(2,1)S(1)} collective-permute-done((bf16[384,768]{1,0:T(8,128)(2,1)S(1)}, bf16[384,768]{1,0:T(8,128)(2,1)S(1)}, u32[]{:S(2)}, u32[]{:S(2)}) %collective-permute-start.28) | collective-permute-done | bytes 589856 | tf_op jit(solution)/shard_map/ppermute | solution.py:529
  381.3 5.0 %collective-permute-done.40 = bf16[96,768]{1,0:T(8,128)(2,1)S(1)} collective-permute-done((bf16[96,768]{1,0:T(8,128)(2,1)S(1)}, bf16[96,768]{1,0:T(8,128)(2,1)S(1)}, u32[]{:S(2)}, u32[]{:S(2)}) %collective-permute-start.40) | collective-permute-done | bytes 147488 | tf_op jit(solution)/shard_map/ppermute | solution.py:534
  386.4 6.0 %collective-permute-start.41 = (bf16[192,768]{1,0:T(8,128)(2,1)S(1)}, bf16[192,768]{1,0:T(8,128)(2,1)S(1)}, u32[]{:S(2)}, u32[]{:S(2)}) collective-permute-start(bf16[192,768]{1,0:T(8,128)(2,1)S(1)} %constant_dynamic-update-slice_fusion.6), channel_id=1, source_target_pairs={{0,8},{1,25},{2,10},{3,27},{4,12},{5,29},{6,14},{7,31},{8,0},{9,17... | collective-permute-start | bytes 884744 | tf_op jit(solution)/shard_map/ppermute | solution.py:534
  393.7 6.0 %collective-permute-done.41 = bf16[192,768]{1,0:T(8,128)(2,1)S(1)} collective-permute-done((bf16[192,768]{1,0:T(8,128)(2,1)S(1)}, bf16[192,768]{1,0:T(8,128)(2,1)S(1)}, u32[]{:S(2)}, u32[]{:S(2)}) %collective-permute-start.41) | collective-permute-done | bytes 294944 | tf_op jit(solution)/shard_map/ppermute | solution.py:534
  404.8 11.3 %collective-permute-done.42 = bf16[384,768]{1,0:T(8,128)(2,1)S(1)} collective-permute-done((bf16[384,768]{1,0:T(8,128)(2,1)S(1)}, bf16[384,768]{1,0:T(8,128)(2,1)S(1)}, u32[]{:S(2)}, u32[]{:S(2)}) %collective-permute-start.42) | collective-permute-done | bytes 589856 | tf_op jit(solution)/shard_map/ppermute | solution.py:534
  417.2 21.0 %collective-permute-start.34 = (bf16[768,768]{1,0:T(8,128)(2,1)S(1)}, bf16[768,768]{1,0:T(8,128)(2,1)S(1)}, u32[]{:S(2)}, u32[]{:S(2)}) collective-permute-start(bf16[768,768]{1,0:T(8,128)(2,1)S(1)} %constant_dynamic-update-slice_fusion.10), channel_id=1, source_target_pairs={{0,8},{1,25},{2,10},{3,27},{4,12},{5,29},{6,14},{7,31},{8,0},{9,17... | collective-permute-start | bytes 3538952 | tf_op jit(solution)/shard_map/ppermute | solution.py:534
  444.1 8.4 %collective-permute-done.34 = bf16[768,768]{1,0:T(8,128)(2,1)S(1)} collective-permute-done((bf16[768,768]{1,0:T(8,128)(2,1)S(1)}, bf16[768,768]{1,0:T(8,128)(2,1)S(1)}, u32[]{:S(2)}, u32[]{:S(2)}) %collective-permute-start.34) | collective-permute-done | bytes 1179680 | tf_op jit(solution)/shard_map/ppermute | solution.py:534
  (263 shorter events, 102.4 us)
Async XLA Ops:
  7.2 313.7 %all-gather.5.cloned.1.call-start = ((), (), s32[]{:S(2)}) async-start(), calls=%async_computation | async-start | bytes 1622016 | tf_op jit(solution)/shard_map/all_gather | solution.py:685
  7.3 35.8 %collective-permute-start = (bf16[3,768,384]{2,1,0:T(8,128)(2,1)}, bf16[3,768,384]{2,1,0:T(8,128)(2,1)}, u32[]{:S(2)}, u32[]{:S(2)}) collective-permute-start(bf16[3,768,384]{2,1,0:T(8,128)(2,1)} %bitcast.53), channel_id=1, source_target_pairs={{0,1},{1,0},{2,3},{3,2},{4,5},{5,4},{6,7},{7,6},{8,9},{9,8},{10,11... | collective-permute-start | bytes 5308424 | tf_op jit(solution)/shard_map/ppermute | solution.py:567
  7.8 52.1 %collective-permute-start.2 = (bf16[768,1536]{1,0:T(8,128)(2,1)}, bf16[768,1536]{1,0:T(8,128)(2,1)}, u32[]{:S(2)}, u32[]{:S(2)}) collective-permute-start(bf16[768,1536]{1,0:T(8,128)(2,1)} %up_a.3), channel_id=1, source_target_pairs={{0,1},{1,0},{2,3},{3,2},{4,5},{5,4},{6,7},{7,6},{8,9},{9,8},{10,11... | collective-permute-start | bytes 7077896 | tf_op jit(solution)/shard_map/ppermute | solution.py:567
  7.9 26.3 %collective-permute-start.3 = (f32[1536]{0:T(1024)}, f32[1536]{0:T(1024)S(1)}, u32[]{:S(2)}, u32[]{:S(2)}) collective-permute-start(f32[1536]{0:T(1024)} %param.26), channel_id=1, source_target_pairs={{0,1},{1,0},{2,3},{3,2},{4,5},{5,4},{6,7},{7,6},{8,9},{9,8},{10,11... | collective-permute-start | bytes 18440 | tf_op jit(solution)/shard_map/ppermute | solution.py:567
  11.0 28.1 %collective-permute-start.5 = (bf16[512,768]{1,0:T(8,128)(2,1)}, bf16[512,768]{1,0:T(8,128)(2,1)}, u32[]{:S(2)}, u32[]{:S(2)}) collective-permute-start(bf16[512,768]{1,0:T(8,128)(2,1)} %get-tuple-element.94), channel_id=1, source_target_pairs={{0,1},{1,0},{2,3},{3,2},{4,5},{5,4},{6,7},{7,6},{8,9},{9,8},{10,11... | collective-permute-start | bytes 2359304 | tf_op jit(solution)/shard_map/ppermute | solution.py:567
  11.1 70.0 %collective-permute-start.4 = (bf16[1536,768]{1,0:T(8,128)(2,1)}, bf16[1536,768]{1,0:T(8,128)(2,1)}, u32[]{:S(2)}, u32[]{:S(2)}) collective-permute-start(bf16[1536,768]{1,0:T(8,128)(2,1)} %down_ref.1), channel_id=1, source_target_pairs={{0,1},{1,0},{2,3},{3,2},{4,5},{5,4},{6,7},{7,6},{8,9},{9,8},{10,11... | collective-permute-start | bytes 7077896 | tf_op jit(solution)/shard_map/ppermute | solution.py:567
  34.2 25.7 %collective-permute-start.1 = (bf16[384,768]{1,0:T(8,128)(2,1)S(1)}, bf16[384,768]{1,0:T(8,128)(2,1)S(1)}, u32[]{:S(2)}, u32[]{:S(2)}) collective-permute-start(bf16[384,768]{1,0:T(8,128)(2,1)S(1)} %copy-done.20), channel_id=1, source_target_pairs={{0,1},{1,0},{2,3},{3,2},{4,5},{5,4},{6,7},{7,6},{8,9},{9,8},{10,11... | collective-permute-start | bytes 1769480 | tf_op jit(solution)/shard_map/ppermute | solution.py:567
  96.0 187.3 %collective-permute-start.35 = (bf16[1536,768]{1,0:T(8,128)(2,1)}, bf16[1536,768]{1,0:T(8,128)(2,1)}, u32[]{:S(2)}, u32[]{:S(2)}) collective-permute-start(bf16[1536,768]{1,0:T(8,128)(2,1)} %get-tuple-element.70), channel_id=1, source_target_pairs={{0,1},{1,0},{2,3},{3,2},{4,5},{5,4},{6,7},{7,6},{8,9},{9,8},{10,11... | collective-permute-start | bytes 7077896 | tf_op jit(solution)/shard_map/ppermute | solution.py:567
  133.6 53.9 %collective-permute-start.17 = (bf16[384,768]{1,0:T(8,128)(2,1)S(1)}, bf16[384,768]{1,0:T(8,128)(2,1)S(1)}, u32[]{:S(2)}, u32[]{:S(2)}) collective-permute-start(bf16[384,768]{1,0:T(8,128)(2,1)S(1)} %convolution_convert_fusion), channel_id=1, source_target_pairs={{0,1},{1,0},{2,3},{3,2},{4,5},{5,4},{6,7},{7,6},{8,9},{9,8},{10,11... | collective-permute-start | bytes 1769480 | tf_op jit(solution)/shard_map/ppermute | solution.py:567
  157.7 123.0 %collective-permute-start.8 = (bf16[3,768,384]{2,1,0:T(8,128)(2,1)}, bf16[3,768,384]{2,1,0:T(8,128)(2,1)}, u32[]{:S(2)}, u32[]{:S(2)}) collective-permute-start(bf16[3,768,384]{2,1,0:T(8,128)(2,1)} %shard_map.268), channel_id=1, source_target_pairs={{0,1},{1,0},{2,3},{3,2},{4,5},{5,4},{6,7},{7,6},{8,9},{9,8},{10,11... | collective-permute-start | bytes 5308424 | tf_op jit(solution)/shard_map/ppermute | solution.py:567
  191.1 81.8 %collective-permute-start.7 = (f32[1,512,768]{2,1,0:T(8,128)}, f32[1,512,768]{2,1,0:T(8,128)}, u32[]{:S(2)}, u32[]{:S(2)}) collective-permute-start(f32[1,512,768]{2,1,0:T(8,128)} %get-tuple-element.91), channel_id=1, source_target_pairs={{0,1},{1,0},{2,3},{3,2},{4,5},{5,4},{6,7},{7,6},{8,9},{9,8},{10,11... | collective-permute-start | bytes 4718600 | tf_op jit(solution)/shard_map/ppermute | solution.py:567
  196.3 13.3 %collective-permute-start.19 = (bf16[96,768]{1,0:T(8,128)(2,1)S(1)}, bf16[96,768]{1,0:T(8,128)(2,1)S(1)}, u32[]{:S(2)}, u32[]{:S(2)}) collective-permute-start(bf16[96,768]{1,0:T(8,128)(2,1)S(1)} %dynamic-slice_convert_fusion.12), channel_id=1, source_target_pairs={{0,4},{1,3},{2,6},{3,1},{4,0},{5,7},{6,2},{7,5},{8,12},{9,11},{10,... | collective-permute-start | bytes 442376 | tf_op jit(solution)/shard_map/ppermute | solution.py:529
  212.2 55.4 %collective-permute-start.6 = (bf16[1,512,768]{2,1,0:T(8,128)(2,1)}, bf16[1,512,768]{2,1,0:T(8,128)(2,1)}, u32[]{:S(2)}, u32[]{:S(2)}) collective-permute-start(bf16[1,512,768]{2,1,0:T(8,128)(2,1)} %get-tuple-element.93), channel_id=1, source_target_pairs={{0,1},{1,0},{2,3},{3,2},{4,5},{5,4},{6,7},{7,6},{8,9},{9,8},{10,11... | collective-permute-start | bytes 2359304 | tf_op jit(solution)/shard_map/ppermute | solution.py:567
  214.7 40.4 %collective-permute-start.21 = (bf16[24,768]{1,0:T(8,128)(2,1)S(1)}, bf16[24,768]{1,0:T(8,128)(2,1)S(1)}, u32[]{:S(2)}, u32[]{:S(2)}) collective-permute-start(bf16[24,768]{1,0:T(8,128)(2,1)S(1)} %dynamic-slice_convert_fusion.15), channel_id=1, source_target_pairs={{0,24},{1,9},{2,26},{3,11},{4,28},{5,13},{6,30},{7,15},{8,16},{9,1... | collective-permute-start | bytes 110600 | tf_op jit(solution)/shard_map/ppermute | solution.py:529
  267.5 21.7 %collective-permute-start.26 = (bf16[2,768,768]{2,1,0:T(8,128)(2,1)}, bf16[2,768,768]{2,1,0:T(8,128)(2,1)S(1)}, u32[]{:S(2)}, u32[]{:S(2)}) collective-permute-start(bf16[2,768,768]{2,1,0:T(8,128)(2,1)} %get-tuple-element.68), channel_id=1, source_target_pairs={{0,1},{1,0},{2,3},{3,2},{4,5},{5,4},{6,7},{7,6},{8,9},{9,8},{10,11... | collective-permute-start | bytes 7077896 | tf_op jit(solution)/shard_map/ppermute | solution.py:567
  283.2 14.5 %collective-permute-start.9 = (bf16[1152,384]{1,0:T(8,128)(2,1)S(1)}, bf16[1152,384]{1,0:T(8,128)(2,1)S(1)}, u32[]{:S(2)}, u32[]{:S(2)}) collective-permute-start(bf16[1152,384]{1,0:T(8,128)(2,1)S(1)} %dynamic-slice_convert_fusion.2), channel_id=1, source_target_pairs={{0,2},{1,5},{2,0},{3,7},{4,6},{5,1},{6,4},{7,3},{8,10},{9,13},{10,... | collective-permute-start | bytes 2654216 | tf_op jit(solution)/shard_map/ppermute | solution.py:529
  287.2 55.2 %collective-permute-start.36 = (bf16[768,768]{1,0:T(8,128)(2,1)}, bf16[768,768]{1,0:T(8,128)(2,1)}, u32[]{:S(2)}, u32[]{:S(2)}) collective-permute-start(bf16[768,768]{1,0:T(8,128)(2,1)} %dynamic-slice_convert_fusion), channel_id=1, source_target_pairs={{0,2},{1,5},{2,0},{3,7},{4,6},{5,1},{6,4},{7,3},{8,10},{9,13},{10,... | collective-permute-start | bytes 3538952 | tf_op jit(solution)/shard_map/ppermute | solution.py:529
  291.0 56.1 %collective-permute-start.27 = (bf16[768,768]{1,0:T(8,128)(2,1)}, bf16[768,768]{1,0:T(8,128)(2,1)}, u32[]{:S(2)}, u32[]{:S(2)}) collective-permute-start(bf16[768,768]{1,0:T(8,128)(2,1)} %dynamic-slice_convert_fusion.1), channel_id=1, source_target_pairs={{0,8},{1,25},{2,10},{3,27},{4,12},{5,29},{6,14},{7,31},{8,0},{9,17... | collective-permute-start | bytes 3538952 | tf_op jit(solution)/shard_map/ppermute | solution.py:529
  298.0 26.7 %collective-permute-start.10 = (bf16[576,384]{1,0:T(8,128)(2,1)S(1)}, bf16[576,384]{1,0:T(8,128)(2,1)}, u32[]{:S(2)}, u32[]{:S(2)}) collective-permute-start(bf16[576,384]{1,0:T(8,128)(2,1)S(1)} %dynamic-slice_convert_fusion.5), channel_id=1, source_target_pairs={{0,4},{1,3},{2,6},{3,1},{4,0},{5,7},{6,2},{7,5},{8,12},{9,11},{10,... | collective-permute-start | bytes 1327112 | tf_op jit(solution)/shard_map/ppermute | solution.py:529
  344.8 11.3 %collective-permute-start.37 = (bf16[384,768]{1,0:T(8,128)(2,1)S(1)}, bf16[384,768]{1,0:T(8,128)(2,1)S(1)}, u32[]{:S(2)}, u32[]{:S(2)}) collective-permute-start(bf16[384,768]{1,0:T(8,128)(2,1)S(1)} %dynamic-slice_convert_fusion.3), channel_id=1, source_target_pairs={{0,4},{1,3},{2,6},{3,1},{4,0},{5,7},{6,2},{7,5},{8,12},{9,11},{10,... | collective-permute-start | bytes 1769480 | tf_op jit(solution)/shard_map/ppermute | solution.py:529
  347.0 8.3 %collective-permute-start.14 = (bf16[288,384]{1,0:T(8,128)(2,1)S(1)}, bf16[288,384]{1,0:T(8,128)(2,1)S(1)}, u32[]{:S(2)}, u32[]{:S(2)}) collective-permute-start(bf16[288,384]{1,0:T(8,128)(2,1)S(1)} %constant_dynamic-update-slice_fusion.30), channel_id=1, source_target_pairs={{0,8},{1,25},{2,10},{3,27},{4,12},{5,29},{6,14},{7,31},{8,0},{9,17... | collective-permute-start | bytes 663560 | tf_op jit(solution)/shard_map/ppermute | solution.py:534
  349.5 18.6 %collective-permute-start.28 = (bf16[384,768]{1,0:T(8,128)(2,1)S(1)}, bf16[384,768]{1,0:T(8,128)(2,1)S(1)}, u32[]{:S(2)}, u32[]{:S(2)}) collective-permute-start(bf16[384,768]{1,0:T(8,128)(2,1)S(1)} %dynamic-slice_convert_fusion.4), channel_id=1, source_target_pairs={{0,24},{1,9},{2,26},{3,11},{4,28},{5,13},{6,30},{7,15},{8,16},{9,1... | collective-permute-start | bytes 1769480 | tf_op jit(solution)/shard_map/ppermute | solution.py:529
  355.4 47.4 %collective-permute-start.15 = (bf16[576,384]{1,0:T(8,128)(2,1)S(1)}, bf16[576,384]{1,0:T(8,128)(2,1)S(1)}, u32[]{:S(2)}, u32[]{:S(2)}) collective-permute-start(bf16[576,384]{1,0:T(8,128)(2,1)S(1)} %constant_dynamic-update-slice_fusion.28), channel_id=1, source_target_pairs={{0,4},{1,3},{2,6},{3,1},{4,0},{5,7},{6,2},{7,5},{8,12},{9,11},{10,... | collective-permute-start | bytes 1327112 | tf_op jit(solution)/shard_map/ppermute | solution.py:534
  356.2 14.9 %collective-permute-start.38 = (bf16[192,768]{1,0:T(8,128)(2,1)S(1)}, bf16[192,768]{1,0:T(8,128)(2,1)S(1)}, u32[]{:S(2)}, u32[]{:S(2)}) collective-permute-start(bf16[192,768]{1,0:T(8,128)(2,1)S(1)} %dynamic-slice_convert_fusion.6), channel_id=1, source_target_pairs={{0,8},{1,25},{2,10},{3,27},{4,12},{5,29},{6,14},{7,31},{8,0},{9,17... | collective-permute-start | bytes 884744 | tf_op jit(solution)/shard_map/ppermute | solution.py:529
  380.5 11.9 %collective-permute-start.31 = (bf16[96,768]{1,0:T(8,128)(2,1)S(1)}, bf16[96,768]{1,0:T(8,128)(2,1)S(1)}, u32[]{:S(2)}, u32[]{:S(2)}) collective-permute-start(bf16[96,768]{1,0:T(8,128)(2,1)S(1)} %get-tuple-element.80), channel_id=1, source_target_pairs={{0,4},{1,3},{2,6},{3,1},{4,0},{5,7},{6,2},{7,5},{8,12},{9,11},{10,... | collective-permute-start | bytes 442376 | tf_op jit(solution)/shard_map/ppermute | solution.py:534
  386.4 13.4 %collective-permute-start.41 = (bf16[192,768]{1,0:T(8,128)(2,1)S(1)}, bf16[192,768]{1,0:T(8,128)(2,1)S(1)}, u32[]{:S(2)}, u32[]{:S(2)}) collective-permute-start(bf16[192,768]{1,0:T(8,128)(2,1)S(1)} %constant_dynamic-update-slice_fusion.6), channel_id=1, source_target_pairs={{0,8},{1,25},{2,10},{3,27},{4,12},{5,29},{6,14},{7,31},{8,0},{9,17... | collective-permute-start | bytes 884744 | tf_op jit(solution)/shard_map/ppermute | solution.py:534
  392.4 8.2 %collective-permute-start.32 = (bf16[192,768]{1,0:T(8,128)(2,1)S(1)}, bf16[192,768]{1,0:T(8,128)(2,1)S(1)}, u32[]{:S(2)}, u32[]{:S(2)}) collective-permute-start(bf16[192,768]{1,0:T(8,128)(2,1)S(1)} %constant_dynamic-update-slice_fusion.14), channel_id=1, source_target_pairs={{0,2},{1,5},{2,0},{3,7},{4,6},{5,1},{6,4},{7,3},{8,10},{9,13},{10,... | collective-permute-start | bytes 884744 | tf_op jit(solution)/shard_map/ppermute | solution.py:534
  399.8 16.3 %collective-permute-start.42 = (bf16[384,768]{1,0:T(8,128)(2,1)S(1)}, bf16[384,768]{1,0:T(8,128)(2,1)S(1)}, u32[]{:S(2)}, u32[]{:S(2)}) collective-permute-start(bf16[384,768]{1,0:T(8,128)(2,1)S(1)} %constant_dynamic-update-slice_fusion.4), channel_id=1, source_target_pairs={{0,4},{1,3},{2,6},{3,1},{4,0},{5,7},{6,2},{7,5},{8,12},{9,11},{10,... | collective-permute-start | bytes 1769480 | tf_op jit(solution)/shard_map/ppermute | solution.py:534
  400.7 16.5 %collective-permute-start.33 = (bf16[384,768]{1,0:T(8,128)(2,1)S(1)}, bf16[384,768]{1,0:T(8,128)(2,1)S(1)}, u32[]{:S(2)}, u32[]{:S(2)}) collective-permute-start(bf16[384,768]{1,0:T(8,128)(2,1)S(1)} %constant_dynamic-update-slice_fusion.12), channel_id=1, source_target_pairs={{0,24},{1,9},{2,26},{3,11},{4,28},{5,13},{6,30},{7,15},{8,16},{9,1... | collective-permute-start | bytes 1769480 | tf_op jit(solution)/shard_map/ppermute | solution.py:534
  402.9 35.7 %collective-permute-start.16 = (bf16[1152,384]{1,0:T(8,128)(2,1)S(1)}, bf16[1152,384]{1,0:T(8,128)(2,1)S(1)}, u32[]{:S(2)}, u32[]{:S(2)}) collective-permute-start(bf16[1152,384]{1,0:T(8,128)(2,1)S(1)} %constant_dynamic-update-slice_fusion.26), channel_id=1, source_target_pairs={{0,2},{1,5},{2,0},{3,7},{4,6},{5,1},{6,4},{7,3},{8,10},{9,13},{10,... | collective-permute-start | bytes 2654216 | tf_op jit(solution)/shard_map/ppermute | solution.py:534
  416.1 25.3 %collective-permute-start.43 = (bf16[768,768]{1,0:T(8,128)(2,1)S(1)}, bf16[768,768]{1,0:T(8,128)(2,1)S(1)}, u32[]{:S(2)}, u32[]{:S(2)}) collective-permute-start(bf16[768,768]{1,0:T(8,128)(2,1)S(1)} %constant_dynamic-update-slice_fusion.2), channel_id=1, source_target_pairs={{0,2},{1,5},{2,0},{3,7},{4,6},{5,1},{6,4},{7,3},{8,10},{9,13},{10,... | collective-permute-start | bytes 3538952 | tf_op jit(solution)/shard_map/ppermute | solution.py:534
  417.2 35.2 %collective-permute-start.34 = (bf16[768,768]{1,0:T(8,128)(2,1)S(1)}, bf16[768,768]{1,0:T(8,128)(2,1)S(1)}, u32[]{:S(2)}, u32[]{:S(2)}) collective-permute-start(bf16[768,768]{1,0:T(8,128)(2,1)S(1)} %constant_dynamic-update-slice_fusion.10), channel_id=1, source_target_pairs={{0,8},{1,25},{2,10},{3,27},{4,12},{5,29},{6,14},{7,31},{8,0},{9,17... | collective-permute-start | bytes 3538952 | tf_op jit(solution)/shard_map/ppermute | solution.py:534
  (43 other events, 284.8 us)
Sparse Core Ops, SparseCore 0:
  263.2 57.6 all-gather.4
